TPU v7x, 32 devices: a whole 2x2x4 slice. The times are simulated.
32 devices in a mesh: dom: 16 (over z, y, core), tile: 2 (over x).
Axes of the slice: x: 2, y: 2, z: 4, core: 2. Of those that a mesh axis runs over, the one named last changes fastest.
Arguments:
- states: float32 [16, 3, 128, 2048], P('dom', None, 'tile'), may hold values from -6 to 6
- offspring: int32 [16], replicated, may hold values from 0 to 4, as said below
- sea_depth: float32 [128, 2048], P('tile'), may hold values from 0.5 to 2
- wind: bfloat16 [6, 2, 64, 1024], P('tile'), may hold values from -6 to 6
- start_hour: int32 [1], replicated, may hold values from 0 to 4
Outputs:
- new_states: float32 [16, 3, 128, 2048], P('dom', None, 'tile')
Inputs may be any that keep to these rules, and one draw needn't show every extreme that they name: offspring counts are whole numbers that sum to 16. The step runs from hour start_hour[0] to the next hour.
All inputs are finite; a program needn't handle non-finite values.
Results may differ from a plain program's by a relative error of at most 0.001.
Values may be sent and summed in bfloat16 or wider, within the bound.
No kernel may reach another device: no remote copies, remote signals or barrier semaphores. Data moves between devices by JAX's collectives and lax.ppermute only.
A program may use at most 128 MiB of HBM per device.

v0:
```python
import functools

import jax
import jax.numpy as jnp
from jax import lax
from jax.experimental import pallas as pl
from jax.experimental.pallas import tpu as pltpu
from jax.sharding import PartitionSpec as P

FRICTION = 0.1
TIME_STEP = 0.4
EDGE = 3
PAD = 8
WIND_VMEM = 10 * 1024 * 1024
STEP_VMEM = 20 * 1024 * 1024
CHUNKS = 2


def parents_by_starts(offspring):
    running = jnp.cumsum(offspring)
    return lambda slots: jnp.sum((running[None, :] <= slots[:, None]).astype(jnp.int32), axis=1)


def parents_by_ends(offspring):
    count = offspring.shape[0]
    index = jnp.arange(count)
    running = jnp.sum(jnp.where(index[None, :] <= index[:, None], offspring[None, :], 0), axis=1)
    return lambda slots: count - jnp.sum(
        (running[None, :] > slots[:, None]).astype(jnp.int32), axis=1
    )


def swap_edges(head, tail):
    count = lax.axis_size("tile")
    me = lax.axis_index("tile")
    above = jnp.zeros_like(head)
    below = jnp.zeros_like(head)
    for parity in range(2):
        pairs = []
        for i in range(parity, count - 1, 2):
            pairs += [(i, i + 1), (i + 1, i)]
        if pairs:
            upper = me % 2 == parity
            got = lax.ppermute(jnp.where(upper, tail, head), "tile", pairs)
            below = jnp.where(upper, got, below)
            above = jnp.where(upper, above, got)
    return above, below


def tall_edge(edge, cols):
    pieces = jnp.concatenate([edge[:, at : at + cols] for at in range(0, edge.shape[1], cols)])
    high = lax.reduce_precision(pieces, 8, 7)
    return [high.astype(jnp.bfloat16), (pieces - high).astype(jnp.bfloat16)]


def wide_edge(tall, rows, pieces):
    size = rows * pieces
    both = wide(tall[:size]) + wide(tall[size : 2 * size])
    return jnp.concatenate([both[at : at + rows] for at in range(0, size, rows)], axis=1)


def surroundings(sea_depth, wind, start_hour):
    count = lax.axis_size("tile")
    devices = lax.axis_size("dom")
    me = lax.axis_index("tile")
    hours_dev, parts, coarse_rows, coarse_cols = wind.shape
    row_count = sea_depth.shape[0]
    own_rows = row_count // 2
    window = min(own_rows + PAD, coarse_rows)
    odd = lax.axis_index("dom") % 2
    hours = [start_hour[0] + odd] if devices % 2 == 0 else [start_hour[0], start_hour[0] + 1]

    def first_row(tile):
        return jnp.clip(tile * own_rows - PAD // 2, 0, coarse_rows - window)

    def panels(tile):
        return [
            lax.dynamic_slice(
                wind, (hour % hours_dev, 0, first_row(tile), 0), (1, parts, window, coarse_cols)
            ).reshape(parts * window, coarse_cols)
            for hour in hours
        ]

    sent = []
    for shift in range(1, count):
        target = (me + shift) % count
        edge = jnp.where(target > me, sea_depth[-EDGE:], sea_depth[:EDGE])
        message = jnp.concatenate(panels(target) + tall_edge(edge, coarse_cols))
        pairs = [(i, (i + shift) % count) for i in range(count)]
        sent.append(lax.ppermute(message, "tile", pairs))
    return jnp.concatenate(panels(me)), sent, hours, first_row(me)


def assembled(sea_depth, wind, around):
    found, sent, hours, _ = around
    count = lax.axis_size("tile")
    devices = lax.axis_size("dom")
    me = lax.axis_index("tile")
    hours_dev = wind.shape[0]
    size = found.shape[0]
    part = size // len(hours)
    pieces = sea_depth.shape[1] // found.shape[1]
    above = jnp.zeros_like(sea_depth[:EDGE])
    below = jnp.zeros_like(sea_depth[:EDGE])
    owner = jnp.concatenate([jnp.full((part, 1), 0) + hour // hours_dev for hour in hours])
    for shift, message in enumerate(sent, 1):
        source = (me - shift) % count
        found = jnp.where(owner == source, message[:size], found)
        edge = wide_edge(message[size:], EDGE, pieces)
        above = jnp.where(source == me - 1, edge, above)
        below = jnp.where(source == me + 1, edge, below)
    if len(hours) == 2:
        return found, above, below
    odd = lax.axis_index("dom") % 2
    other = lax.ppermute(found, "dom", [(i, i ^ 1) for i in range(devices)])
    both = [jnp.where(odd == 0, found, other), jnp.where(odd == 0, other, found)]
    return jnp.concatenate(both), above, below


def wind_kernel(where_ref, coarse_ref, fine_ref):
    hours, parts, rows, fine_cols = fine_ref.shape
    coarse_cols = fine_cols // 2
    window = coarse_ref.shape[0] // (hours * parts)
    first = where_ref[0]
    base = where_ref[1]
    fine_row = lax.broadcasted_iota(jnp.int32, (rows, window), 0) + first
    coarse_row = lax.broadcasted_iota(jnp.int32, (rows, window), 1) + base
    lift = jnp.where((fine_row >> 1) == coarse_row, 1.0, 0.0).astype(jnp.bfloat16)
    step = 128
    fine_col = lax.broadcasted_iota(jnp.int32, (step, 2 * step), 1)
    coarse_col = lax.broadcasted_iota(jnp.int32, (step, 2 * step), 0)
    widen = jnp.where((fine_col >> 1) == coarse_col, 1.0, 0.0).astype(jnp.bfloat16)
    for left in range(0, coarse_cols, step):
        cells = coarse_ref[:, left : left + step]
        wide_cells = jnp.dot(cells, widen, preferred_element_type=jnp.float32)
        for hour in range(hours):
            for part in range(parts):
                low = (hour * parts + part) * window
                panel = wide_cells[low : low + window].astype(jnp.bfloat16)
                tall = jnp.dot(lift, panel, preferred_element_type=jnp.float32)
                fine_ref[hour, part, :, 2 * left : 2 * (left + step)] = TIME_STEP * tall


def fine_wind(coarse, first, base, rows):
    hours, parts = 2, 2
    window, cols = coarse.shape[0] // (hours * parts), coarse.shape[1]
    return pl.pallas_call(
        wind_kernel,
        out_shape=jax.ShapeDtypeStruct((hours, parts, rows, 2 * cols), jnp.float32),
        in_specs=[
            pl.BlockSpec(memory_space=pltpu.SMEM),
            pl.BlockSpec(memory_space=pltpu.VMEM),
        ],
        out_specs=pl.BlockSpec(memory_space=pltpu.VMEM),
        compiler_params=pltpu.CompilerParams(vmem_limit_bytes=WIND_VMEM),
        cost_estimate=pl.CostEstimate(
            flops=4 * hours * parts * rows * window * cols,
            bytes_accessed=8 * hours * parts * rows * cols,
            transcendentals=0,
        ),
    )(jnp.stack([first, base]).astype(jnp.int32), coarse)


def sections(state_ref, depth_ref, wind_at, one, two, flux, base, first, total_rows, store, closed):
    rows = state_ref.shape[1]
    cols = state_ref.shape[2]
    blocks = rows // PAD

    def shifted(ref, index, row, by):
        if 0 <= row + by <= rows - PAD:
            return ref[index, row + by : row + by + PAD, :]
        turned = pltpu.roll(ref[index, row : row + PAD, :], -by % PAD, 0)
        if not closed:
            return turned
        at = lax.broadcasted_iota(jnp.int32, (PAD, 1), 0)
        return jnp.where(at == (0 if by < 0 else PAD - 1), 0.0, turned)

    def across(field):
        return pltpu.roll(field, cols - 1, 1) - pltpu.roll(field, 1, 1)

    def section(source, stress, share, put):
        for block in range(blocks):
            here = pl.ds(block * PAD, PAD)
            there = pl.ds(base + block * PAD, PAD)
            flux[0, here, :] = depth_ref[there, :] * source[2, here, :]
        for block in range(blocks):
            low = block * PAD
            here = pl.ds(low, PAD)
            there = pl.ds(base + low, PAD)
            row = first + low + lax.broadcasted_iota(jnp.int32, (PAD, 1), 0)
            turn = TIME_STEP * (0.1 + 0.4 * row.astype(jnp.float32) / total_rows)
            surface = source[0, here, :]
            east = source[1, here, :]
            north = source[2, here, :]
            flux_up = shifted(flux, 0, low, 1) - shifted(flux, 0, low, -1)
            next_surface = surface - (across(depth_ref[there, :] * east) + flux_up)
            rise = shifted(source, 0, low, 1) - shifted(source, 0, low, -1)
            half = 0.5 * TIME_STEP
            keep = 1.0 - TIME_STEP * FRICTION
            next_east = keep * east + turn * north - half * across(surface) + stress(0, there)
            next_north = keep * north - turn * east - half * rise + stress(1, there)
            values = [next_surface, next_east, next_north]
            if share != 1.0:
                values = [
                    (1.0 - share) * state_ref[part, here, :] + share * value
                    for part, value in enumerate(values)
                ]
            put(block, values)

    def into(target):
        def put(block, values):
            for part, value in enumerate(values):
                target[part, pl.ds(block * PAD, PAD), :] = value

        return put

    section(state_ref, lambda part, there: wind_at[0, part, there, :], 1.0, into(one))
    section(one, lambda part, there: wind_at[1, part, there, :], 0.25, into(two))
    section(
        two,
        lambda part, there: 0.5 * (wind_at[0, part, there, :] + wind_at[1, part, there, :]),
        2.0 / 3.0,
        store,
    )


def step_kernel(total_rows, where_ref, state_ref, depth_ref, wind_ref, out_ref, one, two, flux, done, sems):
    rows = state_ref.shape[1]

    def write(block):
        here = pl.ds(block * PAD, PAD)
        return pltpu.make_async_copy(done.at[:, here], out_ref.at[:, here], sems.at[block])

    def store(block, values):
        for part, value in enumerate(values):
            done[part, pl.ds(block * PAD, PAD), :] = value
        write(block).start()

    first = where_ref[0] + PAD
    sections(
        state_ref, depth_ref, wind_ref, one, two, flux, PAD, first, total_rows, store, True
    )
    for block in range(rows // PAD):
        write(block).wait()


def step(state, depth, wind, first, total_rows):
    parts, rows, cols = state.shape
    vmem = pl.BlockSpec(memory_space=pltpu.VMEM)
    return pl.pallas_call(
        functools.partial(step_kernel, total_rows),
        out_shape=jax.ShapeDtypeStruct((parts, rows, cols), jnp.float32),
        in_specs=[pl.BlockSpec(memory_space=pltpu.SMEM), vmem, vmem, vmem],
        out_specs=pl.BlockSpec(memory_space=pltpu.HBM),
        scratch_shapes=[
            pltpu.VMEM((parts, rows, cols), jnp.float32),
            pltpu.VMEM((parts, rows, cols), jnp.float32),
            pltpu.VMEM((1, rows, cols), jnp.float32),
            pltpu.VMEM((parts, rows, cols), jnp.float32),
            pltpu.SemaphoreType.DMA((rows // PAD,)),
        ],
        compiler_params=pltpu.CompilerParams(vmem_limit_bytes=STEP_VMEM),
        cost_estimate=pl.CostEstimate(
            flops=100 * parts * rows * cols,
            bytes_accessed=4 * (3 * parts + 3) * rows * cols,
            transcendentals=0,
        ),
    )(first[None].astype(jnp.int32), state, depth, wind)


def edge_kernel(
    total_rows, where_ref, above_ref, below_ref, depth_ref, wind_ref, old_ref, out_ref,
    one, two, flux, done, kept, sems,
):
    rows = out_ref.shape[1]
    first = where_ref[0]

    def edge(window, base, block, at, used):
        here = pl.ds(at, PAD)
        read = pltpu.make_async_copy(old_ref.at[:, here], kept, sems.at[0])
        write = pltpu.make_async_copy(done, out_ref.at[:, here], sems.at[1])
        read.start()

        def store(number, values):
            if number != block:
                return
            read.wait()
            row = lax.broadcasted_iota(jnp.int32, (PAD, 1), 0)
            for part, value in enumerate(values):
                done[part] = jnp.where(used(row), value, kept[part])
            write.start()

        sections(
            window, depth_ref, wind_ref, one, two, flux, base, first + base, total_rows, store, False
        )
        write.wait()

    @pl.when(first + PAD > 0)
    def _():
        edge(above_ref, 0, 1, 0, lambda row: row < EDGE)

    @pl.when(first + PAD + rows < total_rows)
    def _():
        edge(below_ref, rows, 0, rows - PAD, lambda row: row >= PAD - EDGE)


def mend(result, above, below, depth, wind, first, total_rows):
    parts, rows, cols = result.shape
    vmem = pl.BlockSpec(memory_space=pltpu.VMEM)
    hbm = pl.BlockSpec(memory_space=pltpu.HBM)
    window = pltpu.VMEM((parts, 2 * PAD, cols), jnp.float32)
    return pl.pallas_call(
        functools.partial(edge_kernel, total_rows),
        out_shape=jax.ShapeDtypeStruct((parts, rows, cols), jnp.float32),
        in_specs=[pl.BlockSpec(memory_space=pltpu.SMEM), vmem, vmem, vmem, vmem, hbm],
        out_specs=hbm,
        scratch_shapes=[
            window,
            window,
            pltpu.VMEM((1, 2 * PAD, cols), jnp.float32),
            pltpu.VMEM((parts, PAD, cols), jnp.float32),
            pltpu.VMEM((parts, PAD, cols), jnp.float32),
            pltpu.SemaphoreType.DMA((2,)),
        ],
        input_output_aliases={5: 0},
        compiler_params=pltpu.CompilerParams(vmem_limit_bytes=STEP_VMEM),
        cost_estimate=pl.CostEstimate(
            flops=200 * parts * PAD * cols,
            bytes_accessed=100 * parts * PAD * cols,
            transcendentals=0,
        ),
    )(first[None].astype(jnp.int32), above, below, depth, wind, result)


def exchange_all(cells, parents):
    spread = lax.all_to_all(cells[None], "dom", split_axis=3, concat_axis=0, tiled=True)
    picked = jnp.take(spread, parents, axis=0)
    return lax.all_to_all(picked, "dom", split_axis=0, concat_axis=3, tiled=True)[0]


def wide(array):
    return array.astype(jnp.float32)


def picked(pools, code):
    units = [pool[unit] for pool in pools for unit in range(2)]
    result = wide(units[0])[None]
    for at, unit in enumerate(units[1:], 1):
        result = jnp.where(code == at, wide(unit)[None], result)
    return result


def once(cells, array):
    row = wide(cells[0, 0, :1, : array.shape[-1]])
    return jnp.where(jnp.abs(row) > 1e30, jnp.zeros_like(array), array)


class Near:
    def __init__(self):
        self.count = lax.axis_size("dom")
        self.groups = self.count // 4
        me = lax.axis_index("dom")
        self.group, self.pair, self.core = me // 4, me // 2 % 2, me % 2
        self.first = self.core == 0
        self.even_group = self.group ^ 1
        self.odd_group = ((self.group + 1) ^ 1) - 1

    def move(self, array, pairs):
        return lax.ppermute(array, "dom", pairs) if pairs else array

    def neighbour(self):
        return [(i, i ^ 1) for i in range(self.count)]

    def across(self, which):
        return [(i, i ^ 2) for i in range(self.count) if i % 2 == which]

    def along(self, which, parity):
        lower = [
            i
            for i in range(self.count - 4)
            if i % 2 == which and i // 4 % 2 == parity
        ]
        return [(i, i + 4) for i in lower] + [(i + 4, i) for i in lower]

    def halves(self, state):
        half = state.shape[1] // 2
        keep = lax.dynamic_slice_in_dim(state, self.core * half, half, 1)
        send = lax.dynamic_slice_in_dim(state, (1 - self.core) * half, half, 1)
        return keep, send.astype(jnp.float16)

    def pair_halves(self, keep, got):
        own = jnp.arange(2).reshape(2, 1, 1, 1) == self.core
        return jnp.where(own, keep[None], wide(got)[None]).astype(jnp.float16)

    def first_round(self, mine):
        one = self.move(mine, self.across(0) + self.along(1, 0))
        two = self.move(mine, self.along(1, 1))
        return mine, one, two

    def held(self, parent):
        place = parent // 4
        in_one = jnp.where(self.first, parent // 2 % 2 != self.pair, place == self.even_group)
        in_two = ~self.first & (place == self.odd_group) & ~in_one
        return parent % 2 + jnp.where(in_two, 4, jnp.where(in_one, 2, 0))

    def codes(self, parents_of):
        first, pair, group = self.first, self.pair, self.group
        entry = jnp.arange(6)
        kind, unit = entry // 2, entry % 2
        unit = jnp.where(kind == 2, unit ^ self.core, unit)
        to_group = jnp.where(kind == 0, jnp.where(first, self.even_group, group), group)
        to_group = jnp.where(kind == 1, self.odd_group, to_group)
        to_pair = jnp.where((kind == 0) & ~first, 1 - pair, pair)
        parent = parents_of(4 * jnp.clip(to_group, 0, self.groups - 1) + 2 * to_pair + unit)
        place = parent // 4
        in_three = jnp.where(first, place == self.even_group, parent // 2 % 2 != pair)
        in_four = first & (place == self.odd_group) & (place != group) & ~in_three
        here = jnp.where(in_three, 6 + unit, jnp.where(in_four, 8 + unit, self.held(parent)))
        code = jnp.where(kind == 2, here, self.held(parent)).reshape(-1, 1, 1, 1)
        return code[:2], code[2:4], code[4:]

    def to_send(self, pools, codes):
        return [picked(pools, code) for code in codes[:2]]

    def second_round(self, even, odd):
        three = self.move(even, self.along(0, 0) + self.across(1))
        return three, self.move(odd, self.along(0, 1))

    def slots(self, pools, codes):
        both = picked(pools, codes[2]).astype(jnp.float16)
        return both[0], both[1]


def body(states, offspring, sea_depth, wind, start_hour):
    row_count = states.shape[2]
    total_rows = row_count * lax.axis_size("tile")
    first = lax.axis_index("tile") * row_count - PAD
    rows = row_count + 2 * PAD
    fill = ((PAD - EDGE, 0), (0, 0)), ((0, PAD - EDGE), (0, 0))
    slots = jnp.arange(offspring.shape[0], dtype=jnp.int32)
    parents = parents_by_starts(offspring)(slots)
    state = states[0]

    def fields(around):
        coarse, above, below = assembled(sea_depth, wind, around)
        depth = (0.5 * TIME_STEP) * jnp.concatenate(
            [jnp.pad(above, fill[0]), sea_depth, jnp.pad(below, fill[1])]
        )
        return depth, fine_wind(coarse, first, around[-1], rows)

    def finish(parts, depth, stress):
        above, below = swap_edges(parts[0][:, :EDGE], parts[-1][:, -EDGE:])
        result = step(
            jnp.concatenate([wide(part) for part in parts], axis=1), depth, stress, first, total_rows
        )
        above = [jnp.pad(wide(above), ((0, 0),) + fill[0]), wide(parts[0][:, :PAD])]
        below = [wide(parts[-1][:, -PAD:]), jnp.pad(wide(below), ((0, 0),) + fill[1])]
        above, below = [jnp.concatenate(window, axis=1) for window in (above, below)]
        return mend(result, above, below, depth, stress, first, total_rows)

    def far():
        around = surroundings(sea_depth, wind, start_hour)
        copied = exchange_all(state.astype(jnp.float16), parents)
        return finish([copied], *fields(around))

    def near():
        plan = Near()
        after = lax.optimization_barrier
        keep, send = after(plan.halves(state))
        got = plan.move(send, plan.neighbour())
        size = keep.shape[1] // CHUNKS
        pools = [
            plan.first_round(plan.pair_halves(keep[:, at : at + size], got[:, at : at + size]))
            for at in range(0, CHUNKS * size, size)
        ]
        mine, near_depth, near_wind, near_offspring = after(
            ([pool[0] for pool in pools], sea_depth, wind, offspring)
        )
        pools = [(own,) + pool[1:] for own, pool in zip(mine, pools)]
        own, sent, *rest = surroundings(near_depth, near_wind, start_hour)
        moved, ready = [None] * CHUNKS, None
        codes = [plan.codes(ways(near_offspring)) for ways in (parents_by_starts, parents_by_ends)]
        for at in reversed(range(CHUNKS)):
            sends = plan.to_send(pools[at], codes[at % 2])
            if ready:
                sends = [once(cells, send) for cells, send in zip(ready, sends)]
            ready = [send.astype(jnp.float16) for send in sends]
            moved[at] = plan.second_round(*ready)
        depth, stress = fields((own, [once(ready[1], message) for message in sent], *rest))
        moved[0], depth, stress = after((moved[0], depth, stress))
        upper, lower = [], []
        for at in range(CHUNKS):
            own, other = plan.slots(pools[at] + moved[at], codes[at % 2])
            got = plan.move(other, plan.neighbour())
            upper.append(jnp.where(plan.first, wide(own), wide(got)).astype(jnp.float16))
            lower.append(jnp.where(plan.first, wide(got), wide(own)).astype(jnp.float16))
        return finish(upper + lower, depth, stress)

    if parents.shape[0] % 4 or row_count % (2 * CHUNKS):
        return far()[None]
    close = jnp.all(jnp.abs(parents // 4 - slots // 4) <= 1)
    return lax.cond(close, near, far)[None]


def solution(mesh):
    return jax.shard_map(
        body,
        mesh=mesh,
        in_specs=(
            P("dom", None, "tile", None),
            P(),
            P("tile", None),
            P("tile", None, None, None),
            P(),
        ),
        out_specs=P("dom", None, "tile", None),
        check_vma=False,
    )
```

profile of v0, /device:TPU:0, one launch (start us, length us, event | category | flops | bytes accessed | tf_op | source)
XLA Modules:
  0.0 42.2 jit_solution(3502848042746276827)
XLA Ops:
  0.0 0.7 %copy.29 = s32[16,1]{1,0:T(8,128)S(1)} copy(s32[16,1]{0,1:T(1,128)} %bitcast.139) | data formatting | bytes 128 | tf_op jit(solution)/shard_map/reshape.200
  1.0 0.7 %compare_reduce_fusion.3 = pred[]{:T(512)} fusion(s32[16]{0:T(128)S(1)} %convert_reduce_fusion.2), kind=kLoop, calls=%fused_computation.235 | loop fusion | flops 431 | bytes 65 | tf_op jit(solution)/shard_map/reduce_and | solution.py:501
  2.3 39.7 %conditional.1 = (f32[1,3,64,2048]{3,2,1,0:T(8,128)}) conditional(s32[]{:T(128)} %convert_element_type.221, (s32[]{:T(128)}, s32[16]{0:T(128)S(1)}, f32[3,64,2048]{2,1,0:T(8,128)}, s32[1]{0:T(128)}, bf16[3,2,64,1024]{3,2,1,0:T(8,128)(2,1)}, /*index=5*/f32[64,2048]{1,0:T(8,128)}) %tuple.96, (s32[]{:T(128)}, f32[3,64,2048]{2,1,0:T(8,128)}, ...), branch_computations={%region_3.4_spmd, %region_4.9_spmd} | conditional | flops 120164016 | bytes 79011016 | solution.py:502
  2.4 1.5 %dynamic-slice_convert_fusion = (f16[3,32,2048]{2,1,0:T(8,128)(2,1)S(1)}, f32[3,32,2048]{2,1,0:T(8,128)S(1)}) fusion(f32[3,64,2048]{2,1,0:T(8,128)} %get-tuple-element.40, s32[]{:T(128)S(6)} %select_n.432, s32[]{:T(128)S(6)} %select_n.431), kind=kLoop, calls=%fused_computation.47 | loop fusion | flops 196608 | bytes 2752520 | tf_op jit(solution)/shard_map/cond/branch_1_fun/convert_element_type | solution.py:389
  3.8 0.5 %collective-permute-start = (f16[3,32,2048]{2,1,0:T(8,128)(2,1)S(1)}, f16[3,32,2048]{2,1,0:T(8,128)(2,1)S(1)}, u32[]{:S(2)}, u32[]{:S(2)}) collective-permute-start(f16[3,32,2048]{2,1,0:T(8,128)(2,1)S(1)} %get-tuple-element.42), channel_id=1, source_target_pairs={{0,2},{2,0},{4,6},{6,4},{8,10},{10,8},{12,14},{14,12},{16,18},{18,... | collective-permute-start | bytes 1179656 | tf_op jit(solution)/shard_map/cond/branch_1_fun/ppermute | solution.py:369
  5.3 0.4 %collective-permute-done = f16[3,32,2048]{2,1,0:T(8,128)(2,1)S(1)} collective-permute-done((f16[3,32,2048]{2,1,0:T(8,128)(2,1)S(1)}, f16[3,32,2048]{2,1,0:T(8,128)(2,1)S(1)}, u32[]{:S(2)}, u32[]{:S(2)}) %collective-permute-start) | collective-permute-done | bytes 393248 | tf_op jit(solution)/shard_map/cond/branch_1_fun/ppermute | solution.py:369
  6.0 0.7 %collective-permute-start.1 = (f16[2,3,16,2048]{3,2,1,0:T(8,128)(2,1)S(1)}, f16[2,3,16,2048]{3,2,1,0:T(8,128)(2,1)S(1)}, u32[]{:S(2)}, u32[]{:S(2)}) collective-permute-start(f16[2,3,16,2048]{3,2,1,0:T(8,128)(2,1)S(1)} %get-tuple-element.47), channel_id=1, source_target_pairs={{10,18},{14,22},{18,10},{22,14},{11,19},{15,23},{19,11},{23,15}} | collective-permute-start | bytes 1179656 | tf_op jit(solution)/shard_map/cond/branch_1_fun/ppermute | solution.py:369
  6.7 3.0 %collective-permute-start.2 = (f16[2,3,16,2048]{3,2,1,0:T(8,128)(2,1)S(1)}, f16[2,3,16,2048]{3,2,1,0:T(8,128)(2,1)S(1)}, u32[]{:S(2)}, u32[]{:S(2)}) collective-permute-start(f16[2,3,16,2048]{3,2,1,0:T(8,128)(2,1)S(1)} %get-tuple-element.47), channel_id=1, source_target_pairs={{0,4},{4,0},{8,12},{12,8},{16,20},{20,16},{24,28},{28,24},{2,10},{... | collective-permute-start | bytes 1179656 | tf_op jit(solution)/shard_map/cond/branch_1_fun/ppermute | solution.py:369
  9.6 0.9 %collective-permute-start.6 = (f16[2,3,16,2048]{3,2,1,0:T(8,128)(2,1)S(1)}, f16[2,3,16,2048]{3,2,1,0:T(8,128)(2,1)S(1)}, u32[]{:S(2)}, u32[]{:S(2)}) collective-permute-start(f16[2,3,16,2048]{3,2,1,0:T(8,128)(2,1)S(1)} %get-tuple-element.48), channel_id=1, source_target_pairs={{10,18},{14,22},{18,10},{22,14},{11,19},{15,23},{19,11},{23,15}} | collective-permute-start | bytes 1179656 | tf_op jit(solution)/shard_map/cond/branch_1_fun/ppermute | solution.py:369
  11.4 1.1 %constant_dynamic-slice_fusion.2 = (bf16[1,2,40,1024]{3,2,1,0:T(8,128)(2,1)S(1)}, bf16[1,2,40,1024]{3,2,1,0:T(8,128)(2,1)S(1)}) fusion(bf16[3,2,64,1024]{3,2,1,0:T(8,128)(2,1)} %get-tuple-element.49, s32[]{:T(128)S(6)} %select_n.508, s32[]{:T(128)} %min.24, s32[]{:T(128)S(6)} %min.23), kind=kLoop, calls=%fused_computation.166 | loop fusion | bytes 655372 | tf_op jit(solution)/shard_map/cond/branch_1_fun/dynamic_slice | solution.py:78
  12.6 2.0 %collective-permute-start.10 = (bf16[92,1024]{1,0:T(8,128)(2,1)S(1)}, bf16[92,1024]{1,0:T(8,128)(2,1)S(1)}, u32[]{:S(2)}, u32[]{:S(2)}) collective-permute-start(bf16[92,1024]{1,0:T(8,128)(2,1)S(1)} %pad_maximum_fusion.5), channel_id=1, source_target_pairs={{0,1},{1,0},{2,3},{3,2},{4,5},{5,4},{6,7},{7,6},{8,9},{9,8},{10,11... | collective-permute-start | bytes 565256 | tf_op jit(solution)/shard_map/cond/branch_1_fun/ppermute | solution.py:90
  14.8 0.6 %collective-permute-done.2 = f16[2,3,16,2048]{3,2,1,0:T(8,128)(2,1)S(1)} collective-permute-done((f16[2,3,16,2048]{3,2,1,0:T(8,128)(2,1)S(1)}, f16[2,3,16,2048]{3,2,1,0:T(8,128)(2,1)S(1)}, u32[]{:S(2)}, u32[]{:S(2)}) %collective-permute-start.2) | collective-permute-done | bytes 393248 | tf_op jit(solution)/shard_map/cond/branch_1_fun/ppermute | solution.py:369
  15.5 0.5 %select_convert_fusion.5 = (f16[2,3,16,2048]{3,2,1,0:T(8,128)(2,1)S(1)}, f16[2,3,16,2048]{3,2,1,0:T(8,128)(2,1)S(1)}) fusion(f32[3,16,2048]{2,1,0:T(8,128)S(1)} %get-tuple-element.116, f32[3,16,2048]{2,1,0:T(8,128)S(1)} %get-tuple-element.115, f32[3,16,2048]{2,1,0:T(8,128)S(1)} %get-tuple-element.114, f32[3,16,2048]{2,1,0:T(8,128)S(1)} %get-tuple-element.113, ...), kind=kLoop, calls=%fused_computation.44 | loop fusion | flops 2359296 | bytes 3145748 | tf_op jit(solution)/shard_map/cond/branch_1_fun/convert_element_type | solution.py:487
  15.9 0.7 %collective-permute-start.3 = (f16[2,3,16,2048]{3,2,1,0:T(8,128)(2,1)S(1)}, f16[2,3,16,2048]{3,2,1,0:T(8,128)(2,1)S(1)}, u32[]{:S(2)}, u32[]{:S(2)}) collective-permute-start(f16[2,3,16,2048]{3,2,1,0:T(8,128)(2,1)S(1)} %get-tuple-element.91), channel_id=1, source_target_pairs={{8,16},{12,20},{16,8},{20,12},{9,17},{13,21},{17,9},{21,13}} | collective-permute-start | bytes 1179656 | tf_op jit(solution)/shard_map/cond/branch_1_fun/ppermute | solution.py:369
  16.6 4.9 %collective-permute-start.4 = (f16[2,3,16,2048]{3,2,1,0:T(8,128)(2,1)S(1)}, f16[2,3,16,2048]{3,2,1,0:T(8,128)(2,1)S(1)}, u32[]{:S(2)}, u32[]{:S(2)}) collective-permute-start(f16[2,3,16,2048]{3,2,1,0:T(8,128)(2,1)S(1)} %get-tuple-element.92), channel_id=1, source_target_pairs={{0,8},{4,12},{16,24},{20,28},{8,0},{12,4},{24,16},{28,20},{2,6},{6... | collective-permute-start | bytes 1179656 | tf_op jit(solution)/shard_map/cond/branch_1_fun/ppermute | solution.py:369
  21.8 0.6 %select_convert_fusion.1 = (f16[2,3,16,2048]{3,2,1,0:T(8,128)(2,1)S(1)}, f16[2,3,16,2048]{3,2,1,0:T(8,128)(2,1)S(1)}) fusion(f32[3,16,2048]{2,1,0:T(8,128)S(1)} %get-tuple-element.122, f32[3,16,2048]{2,1,0:T(8,128)S(1)} %get-tuple-element.121, f32[3,16,2048]{2,1,0:T(8,128)S(1)} %get-tuple-element.120, f32[3,16,2048]{2,1,0:T(8,128)S(1)} %get-tuple-element.119, ...), kind=kLoop, calls=%fused_computation.40 | loop fusion | flops 2752512 | bytes 3149844 | tf_op jit(solution)/shard_map/cond/branch_1_fun/convert_element_type | solution.py:487
  22.4 0.7 %collective-permute-start.9 = (f16[2,3,16,2048]{3,2,1,0:T(8,128)(2,1)S(1)}, f16[2,3,16,2048]{3,2,1,0:T(8,128)(2,1)S(1)}, u32[]{:S(2)}, u32[]{:S(2)}) collective-permute-start(f16[2,3,16,2048]{3,2,1,0:T(8,128)(2,1)S(1)} %get-tuple-element.89), channel_id=1, source_target_pairs={{8,16},{12,20},{16,8},{20,12},{9,17},{13,21},{17,9},{21,13}} | collective-permute-start | bytes 1179656 | tf_op jit(solution)/shard_map/cond/branch_1_fun/ppermute | solution.py:369
  23.3 2.8 %collective-permute-start.8 = (f16[2,3,16,2048]{3,2,1,0:T(8,128)(2,1)S(1)}, f16[2,3,16,2048]{3,2,1,0:T(8,128)(2,1)S(1)}, u32[]{:S(2)}, u32[]{:S(2)}) collective-permute-start(f16[2,3,16,2048]{3,2,1,0:T(8,128)(2,1)S(1)} %get-tuple-element.90), channel_id=1, source_target_pairs={{0,8},{4,12},{16,24},{20,28},{8,0},{12,4},{24,16},{28,20},{2,6},{6... | collective-permute-start | bytes 1179656 | tf_op jit(solution)/shard_map/cond/branch_1_fun/ppermute | solution.py:369
  26.3 2.1 %branch_1_fun.3.wind_ref = f32[2,2,80,2048]{3,2,1,0:T(8,128)S(1)} custom-call(s32[2]{0:T(128)S(1)} %pad_add_fusion.1.where_ref, bf16[160,1024]{1,0:T(8,128)(2,1)S(1)} %pad_maximum_fusion.4.coarse_ref), custom_call_target="tpu_custom_call" | custom-call | flops 52428800 | bytes 2621440 | tf_op jit(solution)/shard_map/cond/branch_1_fun/pallas_call | solution.py:147
  29.1 2.7 %collective-permute-done.8 = f16[2,3,16,2048]{3,2,1,0:T(8,128)(2,1)S(1)} collective-permute-done((f16[2,3,16,2048]{3,2,1,0:T(8,128)(2,1)S(1)}, f16[2,3,16,2048]{3,2,1,0:T(8,128)(2,1)S(1)}, u32[]{:S(2)}, u32[]{:S(2)}) %collective-permute-start.8) | collective-permute-done | bytes 393248 | tf_op jit(solution)/shard_map/cond/branch_1_fun/ppermute | solution.py:369
  32.7 1.3 %collective-permute-done.12 = f16[3,16,2048]{2,1,0:T(8,128)(2,1)S(1)} collective-permute-done((f16[3,16,2048]{2,1,0:T(8,128)(2,1)S(1)}, f16[3,16,2048]{2,1,0:T(8,128)(2,1)S(1)}, u32[]{:S(2)}, u32[]{:S(2)}) %collective-permute-start.12) | collective-permute-done | bytes 196640 | tf_op jit(solution)/shard_map/cond/branch_1_fun/ppermute | solution.py:369
  34.2 1.6 %collective-permute-start.13 = (f16[3,3,2048]{2,1,0:T(4,128)(2,1)S(1)}, f16[3,3,2048]{2,1,0:T(4,128)(2,1)S(1)}, u32[]{:S(2)}, u32[]{:S(2)}) collective-permute-start(f16[3,3,2048]{2,1,0:T(4,128)(2,1)S(1)} %slice_select_fusion.4), channel_id=1, source_target_pairs={{0,1},{1,0},{2,3},{3,2},{4,5},{5,4},{6,7},{7,6},{8,9},{9,8},{10,11... | collective-permute-start | bytes 110600 | tf_op jit(solution)/shard_map/cond/branch_1_fun/ppermute | solution.py:44
  36.0 3.5 %branch_1_fun.4.old_ref = f32[3,64,2048]{2,1,0:T(8,128)} custom-call(s32[1]{0:T(128)} %bitcast.14.where_ref, f32[3,64,2048]{2,1,0:T(8,128)S(1)} %maximum_convert_fusion.state_ref, f32[80,2048]{1,0:T(8,128)S(1)} %fusion.10.depth_ref, f32[2,2,80,2048]{3,2,1,0:T(8,128)S(1)} %branch_1_fun.3.wind_ref), custom_call_target="tpu_custom_call" | custom-call | flops 39321600 | bytes 6291456 | tf_op jit(solution)/shard_map/cond/branch_1_fun/pallas_call | solution.py:250
  39.7 2.1 %branch_1_fun.5 = f32[3,64,2048]{2,1,0:T(8,128)} custom-call(s32[1]{0:T(128)} %bitcast.14.where_ref, f32[3,16,2048]{2,1,0:T(8,128)S(1)} %fusion.20.above_ref, f32[3,16,2048]{2,1,0:T(8,128)S(1)} %fusion.18.below_ref, f32[80,2048]{1,0:T(8,128)S(1)} %fusion.10.depth_ref, f32[2,2,80,2048]{3,2,1,0:T(8,128)S(1)} %branch_1_fun.3.wind_ref, ...), custom_call_target="tpu_custom_call", output_to_operand_aliasing={{}: (5, {})} | custom-call | flops 9830400 | bytes 4915200 | tf_op jit(solution)/shard_map/cond/branch_1_fun/pallas_call | solution.py:312
  (73 shorter events, 4.3 us)
Async XLA Ops:
  3.8 1.9 %collective-permute-start = (f16[3,32,2048]{2,1,0:T(8,128)(2,1)S(1)}, f16[3,32,2048]{2,1,0:T(8,128)(2,1)S(1)}, u32[]{:S(2)}, u32[]{:S(2)}) collective-permute-start(f16[3,32,2048]{2,1,0:T(8,128)(2,1)S(1)} %get-tuple-element.42), channel_id=1, source_target_pairs={{0,2},{2,0},{4,6},{6,4},{8,10},{10,8},{12,14},{14,12},{16,18},{18,... | collective-permute-start | bytes 1179656 | tf_op jit(solution)/shard_map/cond/branch_1_fun/ppermute | solution.py:369
  5.3 5.3 %copy-start.3 = (s32[16]{0:T(128)S(1)}, s32[16]{0:T(128)}, u32[]{:S(2)}) copy-start(s32[16]{0:T(128)} %get-tuple-element.46) | copy-start | bytes 196 | tf_op jit(solution)/shard_map/cond
  5.8 5.6 %copy-start.1 = (f32[64,2048]{1,0:T(8,128)S(1)}, f32[64,2048]{1,0:T(8,128)}, u32[]{:S(2)}) copy-start(f32[64,2048]{1,0:T(8,128)} %get-tuple-element.51) | copy-start | bytes 1572868 | tf_op jit(solution)/shard_map/cond
  6.0 8.7 %collective-permute-start.1 = (f16[2,3,16,2048]{3,2,1,0:T(8,128)(2,1)S(1)}, f16[2,3,16,2048]{3,2,1,0:T(8,128)(2,1)S(1)}, u32[]{:S(2)}, u32[]{:S(2)}) collective-permute-start(f16[2,3,16,2048]{3,2,1,0:T(8,128)(2,1)S(1)} %get-tuple-element.47), channel_id=1, source_target_pairs={{10,18},{14,22},{18,10},{22,14},{11,19},{15,23},{19,11},{23,15}} | collective-permute-start | bytes 1179656 | tf_op jit(solution)/shard_map/cond/branch_1_fun/ppermute | solution.py:369
  6.7 8.7 %collective-permute-start.2 = (f16[2,3,16,2048]{3,2,1,0:T(8,128)(2,1)S(1)}, f16[2,3,16,2048]{3,2,1,0:T(8,128)(2,1)S(1)}, u32[]{:S(2)}, u32[]{:S(2)}) collective-permute-start(f16[2,3,16,2048]{3,2,1,0:T(8,128)(2,1)S(1)} %get-tuple-element.47), channel_id=1, source_target_pairs={{0,4},{4,0},{8,12},{12,8},{16,20},{20,16},{24,28},{28,24},{2,10},{... | collective-permute-start | bytes 1179656 | tf_op jit(solution)/shard_map/cond/branch_1_fun/ppermute | solution.py:369
  9.6 12.0 %collective-permute-start.6 = (f16[2,3,16,2048]{3,2,1,0:T(8,128)(2,1)S(1)}, f16[2,3,16,2048]{3,2,1,0:T(8,128)(2,1)S(1)}, u32[]{:S(2)}, u32[]{:S(2)}) collective-permute-start(f16[2,3,16,2048]{3,2,1,0:T(8,128)(2,1)S(1)} %get-tuple-element.48), channel_id=1, source_target_pairs={{10,18},{14,22},{18,10},{22,14},{11,19},{15,23},{19,11},{23,15}} | collective-permute-start | bytes 1179656 | tf_op jit(solution)/shard_map/cond/branch_1_fun/ppermute | solution.py:369
  10.5 11.2 %collective-permute-start.7 = (f16[2,3,16,2048]{3,2,1,0:T(8,128)(2,1)S(1)}, f16[2,3,16,2048]{3,2,1,0:T(8,128)(2,1)S(1)}, u32[]{:S(2)}, u32[]{:S(2)}) collective-permute-start(f16[2,3,16,2048]{3,2,1,0:T(8,128)(2,1)S(1)} %get-tuple-element.48), channel_id=1, source_target_pairs={{0,4},{4,0},{8,12},{12,8},{16,20},{20,16},{24,28},{28,24},{2,10},{... | collective-permute-start | bytes 1179656 | tf_op jit(solution)/shard_map/cond/branch_1_fun/ppermute | solution.py:369
  12.6 10.6 %collective-permute-start.10 = (bf16[92,1024]{1,0:T(8,128)(2,1)S(1)}, bf16[92,1024]{1,0:T(8,128)(2,1)S(1)}, u32[]{:S(2)}, u32[]{:S(2)}) collective-permute-start(bf16[92,1024]{1,0:T(8,128)(2,1)S(1)} %pad_maximum_fusion.5), channel_id=1, source_target_pairs={{0,1},{1,0},{2,3},{3,2},{4,5},{5,4},{6,7},{7,6},{8,9},{9,8},{10,11... | collective-permute-start | bytes 565256 | tf_op jit(solution)/shard_map/cond/branch_1_fun/ppermute | solution.py:90
  15.9 12.5 %collective-permute-start.3 = (f16[2,3,16,2048]{3,2,1,0:T(8,128)(2,1)S(1)}, f16[2,3,16,2048]{3,2,1,0:T(8,128)(2,1)S(1)}, u32[]{:S(2)}, u32[]{:S(2)}) collective-permute-start(f16[2,3,16,2048]{3,2,1,0:T(8,128)(2,1)S(1)} %get-tuple-element.91), channel_id=1, source_target_pairs={{8,16},{12,20},{16,8},{20,12},{9,17},{13,21},{17,9},{21,13}} | collective-permute-start | bytes 1179656 | tf_op jit(solution)/shard_map/cond/branch_1_fun/ppermute | solution.py:369
  16.6 11.9 %collective-permute-start.4 = (f16[2,3,16,2048]{3,2,1,0:T(8,128)(2,1)S(1)}, f16[2,3,16,2048]{3,2,1,0:T(8,128)(2,1)S(1)}, u32[]{:S(2)}, u32[]{:S(2)}) collective-permute-start(f16[2,3,16,2048]{3,2,1,0:T(8,128)(2,1)S(1)} %get-tuple-element.92), channel_id=1, source_target_pairs={{0,8},{4,12},{16,24},{20,28},{8,0},{12,4},{24,16},{28,20},{2,6},{6... | collective-permute-start | bytes 1179656 | tf_op jit(solution)/shard_map/cond/branch_1_fun/ppermute | solution.py:369
  22.4 9.5 %collective-permute-start.9 = (f16[2,3,16,2048]{3,2,1,0:T(8,128)(2,1)S(1)}, f16[2,3,16,2048]{3,2,1,0:T(8,128)(2,1)S(1)}, u32[]{:S(2)}, u32[]{:S(2)}) collective-permute-start(f16[2,3,16,2048]{3,2,1,0:T(8,128)(2,1)S(1)} %get-tuple-element.89), channel_id=1, source_target_pairs={{8,16},{12,20},{16,8},{20,12},{9,17},{13,21},{17,9},{21,13}} | collective-permute-start | bytes 1179656 | tf_op jit(solution)/shard_map/cond/branch_1_fun/ppermute | solution.py:369
  23.2 3.0 %collective-permute-start.11 = (bf16[80,1024]{1,0:T(8,128)(2,1)S(1)}, bf16[80,1024]{1,0:T(8,128)(2,1)S(1)}, u32[]{:S(2)}, u32[]{:S(2)}) collective-permute-start(bf16[80,1024]{1,0:T(8,128)(2,1)S(1)} %slice_select_fusion.3), channel_id=1, source_target_pairs={{0,2},{2,0},{4,6},{6,4},{8,10},{10,8},{12,14},{14,12},{16,18},{18,... | collective-permute-start | bytes 491528 | tf_op jit(solution)/shard_map/cond/branch_1_fun/ppermute | solution.py:115
  23.3 8.6 %collective-permute-start.8 = (f16[2,3,16,2048]{3,2,1,0:T(8,128)(2,1)S(1)}, f16[2,3,16,2048]{3,2,1,0:T(8,128)(2,1)S(1)}, u32[]{:S(2)}, u32[]{:S(2)}) collective-permute-start(f16[2,3,16,2048]{3,2,1,0:T(8,128)(2,1)S(1)} %get-tuple-element.90), channel_id=1, source_target_pairs={{0,8},{4,12},{16,24},{20,28},{8,0},{12,4},{24,16},{28,20},{2,6},{6... | collective-permute-start | bytes 1179656 | tf_op jit(solution)/shard_map/cond/branch_1_fun/ppermute | solution.py:369
  29.1 3.5 %collective-permute-start.5 = (f16[3,16,2048]{2,1,0:T(8,128)(2,1)S(1)}, f16[3,16,2048]{2,1,0:T(8,128)(2,1)S(1)}, u32[]{:S(2)}, u32[]{:S(2)}) collective-permute-start(f16[3,16,2048]{2,1,0:T(8,128)(2,1)S(1)} %slice_bitcast_fusion.7), channel_id=1, source_target_pairs={{0,2},{2,0},{4,6},{6,4},{8,10},{10,8},{12,14},{14,12},{16,18},{18,... | collective-permute-start | bytes 589832 | tf_op jit(solution)/shard_map/cond/branch_1_fun/ppermute | solution.py:369
  32.5 1.5 %collective-permute-start.12 = (f16[3,16,2048]{2,1,0:T(8,128)(2,1)S(1)}, f16[3,16,2048]{2,1,0:T(8,128)(2,1)S(1)}, u32[]{:S(2)}, u32[]{:S(2)}) collective-permute-start(f16[3,16,2048]{2,1,0:T(8,128)(2,1)S(1)} %slice_bitcast_fusion), channel_id=1, source_target_pairs={{0,2},{2,0},{4,6},{6,4},{8,10},{10,8},{12,14},{14,12},{16,18},{18,... | collective-permute-start | bytes 589832 | tf_op jit(solution)/shard_map/cond/branch_1_fun/ppermute | solution.py:369
  34.2 5.4 %collective-permute-start.13 = (f16[3,3,2048]{2,1,0:T(4,128)(2,1)S(1)}, f16[3,3,2048]{2,1,0:T(4,128)(2,1)S(1)}, u32[]{:S(2)}, u32[]{:S(2)}) collective-permute-start(f16[3,3,2048]{2,1,0:T(4,128)(2,1)S(1)} %slice_select_fusion.4), channel_id=1, source_target_pairs={{0,1},{1,0},{2,3},{3,2},{4,5},{5,4},{6,7},{7,6},{8,9},{9,8},{10,11... | collective-permute-start | bytes 110600 | tf_op jit(solution)/shard_map/cond/branch_1_fun/ppermute | solution.py:44
where the time goes:
time: 42.5 us; the launch traced here: 42.2 us
  starting transfers between devices  18 us (42%)
  Pallas kernels  7.77 us (18%)
  other arithmetic  6.86 us (16%)
  waiting for transfers between devices  5.1 us (12%)
  local copies, waits for them, and re-layouts  2.12 us (5%)
  loops' own time  1.51 us (4%)
  between operations  0.84 us (2%)
    ppermute x11, starting transfers between devices, move(): return lax.ppermute(array, 'dom', pairs) if pairs else array  14.4 us
    ppermute x11, waiting for transfers between devices, move(): return lax.ppermute(array, 'dom', pairs) if pairs else array  5.09 us
    pallas_call x1, Pallas kernels, step(): pl.pallas_call(functools.partial(step_kernel, total_rows), out_shape=jax....  3.55 us
    pallas_call x1, Pallas kernels, fine_wind(): pl.pallas_call(wind_kernel, out_shape=jax.ShapeDtypeStruct((hours, parts,...  2.13 us
    pallas_call x1, Pallas kernels, mend(): pl.pallas_call(functools.partial(edge_kernel, total_rows), out_shape=jax....  2.09 us
    ppermute x1, starting transfers between devices, surroundings(): sent.append(lax.ppermute(message, 'tile', pairs))  2.03 us
    ppermute x1, starting transfers between devices, swap_edges(): got = lax.ppermute(jnp.where(upper, tail, head), 'tile', pairs)  1.56 us
    another operation x1, loops' own time, body(): return lax.cond(close, near, far)[None]  1.51 us
  transfers between devices with their start and end apart: 14, of which 4 were waited for; matrix products, arithmetic and copies ran while one was open for 13% of the time, Pallas kernels for 13%

commit v1 on v0

--- a/solution.py
+++ b/solution.py
@@ -334,7 +334,7 @@
 
 def exchange_all(cells, parents):
     spread = lax.all_to_all(cells[None], "dom", split_axis=3, concat_axis=0, tiled=True)
-    picked = jnp.take(spread, parents, axis=0)
+    picked = jnp.take(spread, parents, axis=0, mode="clip")
     return lax.all_to_all(picked, "dom", split_axis=0, concat_axis=3, tiled=True)[0]
 
 
@@ -438,7 +438,6 @@
     rows = row_count + 2 * PAD
     fill = ((PAD - EDGE, 0), (0, 0)), ((0, PAD - EDGE), (0, 0))
     slots = jnp.arange(offspring.shape[0], dtype=jnp.int32)
-    parents = parents_by_starts(offspring)(slots)
     state = states[0]
 
     def fields(around):
@@ -460,6 +459,7 @@
 
     def far():
         around = surroundings(sea_depth, wind, start_hour)
+        parents = parents_by_starts(offspring)(slots)
         copied = exchange_all(state.astype(jnp.float16), parents)
         return finish([copied], *fields(around))
 
@@ -496,9 +496,11 @@
             lower.append(jnp.where(plan.first, wide(got), wide(own)).astype(jnp.float16))
         return finish(upper + lower, depth, stress)
 
-    if parents.shape[0] % 4 or row_count % (2 * CHUNKS):
+    if slots.shape[0] % 4 or row_count % (2 * CHUNKS):
         return far()[None]
-    close = jnp.all(jnp.abs(parents // 4 - slots // 4) <= 1)
+    ends = 4 * (1 + slots[: slots.shape[0] // 4])
+    copies = jnp.sum(jnp.where(slots[None, :] < ends[:, None], offspring[None, :], 0), axis=1)
+    close = jnp.all(jnp.abs(copies - ends) <= 4)
     return lax.cond(close, near, far)[None]
 
 

time: 42.5 us -> 41.6 us (0.979)
  local copies, waits for them, and re-layouts: 2.12 us -> 1.39 us
  waiting for transfers between devices: 5.1 us -> 4.42 us
  other arithmetic: 6.86 us -> 7.42 us
    another operation x2 -> x1, local copies, waits for them, and re-layouts: 0.81 us -> 0.08 us
    reduce_sum x1, other arithmetic: 0.12 us -> 0.84 us  [body(): jnp.sum(jnp.where(slots[None, :] < ends[:, None], offspring[None, :], 0),...]
    ppermute x11, waiting for transfers between devices: 5.09 us -> 4.42 us  [move(): return lax.ppermute(array, 'dom', pairs) if pairs else array]
    ppermute x1, starting transfers between devices: 0.07 us -> 0.64 us  [assembled(): other = lax.ppermute(found, 'dom', [(i, i ^ 1) for i in range(devices)])]
    ppermute x11, starting transfers between devices: 14.4 us -> 13.8 us  [move(): return lax.ppermute(array, 'dom', pairs) if pairs else array]
  transfers between devices with their start and end apart: 14 -> 14, of which waited for: 4 -> 3; matrix products, arithmetic and copies ran while one was open for 13% -> 13% of each run, Pallas kernels for 13% -> 14%
where the time goes in v1:
time: 41.6 us; the launch traced here: 41.4 us
  starting transfers between devices  18 us (43%)
  Pallas kernels  7.76 us (19%)
  other arithmetic  7.42 us (18%)
  waiting for transfers between devices  4.42 us (11%)
  loops' own time  1.48 us (4%)
  local copies, waits for them, and re-layouts  1.39 us (3%)
  between operations  0.84 us (2%)
    ppermute x11, starting transfers between devices, move(): return lax.ppermute(array, 'dom', pairs) if pairs else array  13.8 us
    ppermute x11, waiting for transfers between devices, move(): return lax.ppermute(array, 'dom', pairs) if pairs else array  4.42 us
    pallas_call x1, Pallas kernels, step(): pl.pallas_call(functools.partial(step_kernel, total_rows), out_shape=jax....  3.55 us
    pallas_call x1, Pallas kernels, fine_wind(): pl.pallas_call(wind_kernel, out_shape=jax.ShapeDtypeStruct((hours, parts,...  2.12 us
    pallas_call x1, Pallas kernels, mend(): pl.pallas_call(functools.partial(edge_kernel, total_rows), out_shape=jax....  2.09 us
    ppermute x1, starting transfers between devices, surroundings(): sent.append(lax.ppermute(message, 'tile', pairs))  2.03 us
    ppermute x1, starting transfers between devices, swap_edges(): got = lax.ppermute(jnp.where(upper, tail, head), 'tile', pairs)  1.56 us
    another operation x1, loops' own time, body(): return lax.cond(close, near, far)[None]  1.48 us
  transfers between devices with their start and end apart: 14, of which 3 were waited for; matrix products, arithmetic and copies ran while one was open for 13% of the time, Pallas kernels for 14%

profile of v1, /device:TPU:0, one launch (start us, length us, event | category | flops | bytes accessed | tf_op | source)
XLA Modules:
  0.0 41.4 jit_solution(13624996927863119102)
XLA Ops:
  0.0 0.8 %select_reduce_fusion.1 = s32[4]{0:T(128)S(1)} fusion(s32[16]{0:T(128)} %param.8, s32[4]{0:T(128)S(1)} %add_multiply_fusion), kind=kLoop, calls=%fused_computation.231 | loop fusion | flops 188 | bytes 96 | tf_op jit(solution)/shard_map/reduce_sum | solution.py:502
  0.8 0.6 %compare_reduce_fusion.3 = pred[]{:T(512)} fusion(s32[4]{0:T(128)S(1)} %select_reduce_fusion.1, s32[16]{0:T(128)S(1)} %iota.43), kind=kLoop, calls=%fused_computation.233 | loop fusion | flops 23 | bytes 33 | tf_op jit(solution)/shard_map/reduce_and | solution.py:503
  2.1 39.0 %conditional.1 = (f32[1,3,64,2048]{3,2,1,0:T(8,128)}) conditional(s32[]{:T(128)} %convert_element_type.220, (s32[]{:T(128)}, f32[3,64,2048]{2,1,0:T(8,128)}, s32[16]{0:T(128)}, s32[16]{0:T(128)S(1)}, s32[1]{0:T(128)}, /*index=5*/bf16[3,2,64,1024]{3,2,1,0:T(8,128)(2,1)}, f32[64,2048]{1,0:T(8,128)}) %tuple.96, (s32[]{:T(128)}, ...), branch_computations={%region_2.5_spmd, %region_5.10_spmd} | conditional | flops 120164016 | bytes 79011016 | solution.py:504
  2.2 1.5 %dynamic-slice_convert_fusion = (f16[3,32,2048]{2,1,0:T(8,128)(2,1)S(1)}, f32[3,32,2048]{2,1,0:T(8,128)S(1)}) fusion(f32[3,64,2048]{2,1,0:T(8,128)} %get-tuple-element.43, s32[]{:T(128)S(6)} %select_n.421, s32[]{:T(128)S(6)} %select_n.420), kind=kLoop, calls=%fused_computation.10 | loop fusion | flops 196608 | bytes 2752520 | tf_op jit(solution)/shard_map/cond/branch_1_fun/convert_element_type | solution.py:389
  3.7 0.5 %collective-permute-start = (f16[3,32,2048]{2,1,0:T(8,128)(2,1)S(1)}, f16[3,32,2048]{2,1,0:T(8,128)(2,1)S(1)}, u32[]{:S(2)}, u32[]{:S(2)}) collective-permute-start(f16[3,32,2048]{2,1,0:T(8,128)(2,1)S(1)} %get-tuple-element.45), channel_id=1, source_target_pairs={{0,2},{2,0},{4,6},{6,4},{8,10},{10,8},{12,14},{14,12},{16,18},{18,... | collective-permute-start | bytes 1179656 | tf_op jit(solution)/shard_map/cond/branch_1_fun/ppermute | solution.py:369
  5.1 0.4 %collective-permute-done = f16[3,32,2048]{2,1,0:T(8,128)(2,1)S(1)} collective-permute-done((f16[3,32,2048]{2,1,0:T(8,128)(2,1)S(1)}, f16[3,32,2048]{2,1,0:T(8,128)(2,1)S(1)}, u32[]{:S(2)}, u32[]{:S(2)}) %collective-permute-start) | collective-permute-done | bytes 393248 | tf_op jit(solution)/shard_map/cond/branch_1_fun/ppermute | solution.py:369
  5.8 3.0 %collective-permute-start.2 = (f16[2,3,16,2048]{3,2,1,0:T(8,128)(2,1)S(1)}, f16[2,3,16,2048]{3,2,1,0:T(8,128)(2,1)S(1)}, u32[]{:S(2)}, u32[]{:S(2)}) collective-permute-start(f16[2,3,16,2048]{3,2,1,0:T(8,128)(2,1)S(1)} %get-tuple-element.50), channel_id=1, source_target_pairs={{0,4},{4,0},{8,12},{12,8},{16,20},{20,16},{24,28},{28,24},{2,10},{... | collective-permute-start | bytes 1179656 | tf_op jit(solution)/shard_map/cond/branch_1_fun/ppermute | solution.py:369
  8.8 0.7 %collective-permute-start.1 = (f16[2,3,16,2048]{3,2,1,0:T(8,128)(2,1)S(1)}, f16[2,3,16,2048]{3,2,1,0:T(8,128)(2,1)S(1)}, u32[]{:S(2)}, u32[]{:S(2)}) collective-permute-start(f16[2,3,16,2048]{3,2,1,0:T(8,128)(2,1)S(1)} %get-tuple-element.50), channel_id=1, source_target_pairs={{10,18},{14,22},{18,10},{22,14},{11,19},{15,23},{19,11},{23,15}} | collective-permute-start | bytes 1179656 | tf_op jit(solution)/shard_map/cond/branch_1_fun/ppermute | solution.py:369
  9.5 0.9 %collective-permute-start.6 = (f16[2,3,16,2048]{3,2,1,0:T(8,128)(2,1)S(1)}, f16[2,3,16,2048]{3,2,1,0:T(8,128)(2,1)S(1)}, u32[]{:S(2)}, u32[]{:S(2)}) collective-permute-start(f16[2,3,16,2048]{3,2,1,0:T(8,128)(2,1)S(1)} %get-tuple-element.51), channel_id=1, source_target_pairs={{10,18},{14,22},{18,10},{22,14},{11,19},{15,23},{19,11},{23,15}} | collective-permute-start | bytes 1179656 | tf_op jit(solution)/shard_map/cond/branch_1_fun/ppermute | solution.py:369
  11.2 1.1 %constant_dynamic-slice_fusion = (bf16[1,2,40,1024]{3,2,1,0:T(8,128)(2,1)S(1)}, bf16[1,2,40,1024]{3,2,1,0:T(8,128)(2,1)S(1)}) fusion(bf16[3,2,64,1024]{3,2,1,0:T(8,128)(2,1)} %get-tuple-element.52, s32[]{:T(128)S(6)} %select_n.497, s32[]{:T(128)} %min.24, s32[]{:T(128)S(6)} %min.23), kind=kLoop, calls=%fused_computation.129 | loop fusion | bytes 655372 | tf_op jit(solution)/shard_map/cond/branch_1_fun/dynamic_slice | solution.py:78
  12.4 2.0 %collective-permute-start.10 = (bf16[92,1024]{1,0:T(8,128)(2,1)S(1)}, bf16[92,1024]{1,0:T(8,128)(2,1)S(1)}, u32[]{:S(2)}, u32[]{:S(2)}) collective-permute-start(bf16[92,1024]{1,0:T(8,128)(2,1)S(1)} %pad_maximum_fusion.1), channel_id=1, source_target_pairs={{0,1},{1,0},{2,3},{3,2},{4,5},{5,4},{6,7},{7,6},{8,9},{9,8},{10,11... | collective-permute-start | bytes 565256 | tf_op jit(solution)/shard_map/cond/branch_1_fun/ppermute | solution.py:90
  14.7 0.5 %select_convert_fusion.5 = (f16[2,3,16,2048]{3,2,1,0:T(8,128)(2,1)S(1)}, f16[2,3,16,2048]{3,2,1,0:T(8,128)(2,1)S(1)}) fusion(f32[3,16,2048]{2,1,0:T(8,128)S(1)} %get-tuple-element.103, f32[3,16,2048]{2,1,0:T(8,128)S(1)} %get-tuple-element.102, f32[3,16,2048]{2,1,0:T(8,128)S(1)} %get-tuple-element.101, f32[3,16,2048]{2,1,0:T(8,128)S(1)} %get-tuple-element.100, ...), kind=kLoop, calls=%fused_computation.7 | loop fusion | flops 2359296 | bytes 3145748 | tf_op jit(solution)/shard_map/cond/branch_1_fun/convert_element_type | solution.py:487
  15.2 0.7 %collective-permute-start.3 = (f16[2,3,16,2048]{3,2,1,0:T(8,128)(2,1)S(1)}, f16[2,3,16,2048]{3,2,1,0:T(8,128)(2,1)S(1)}, u32[]{:S(2)}, u32[]{:S(2)}) collective-permute-start(f16[2,3,16,2048]{3,2,1,0:T(8,128)(2,1)S(1)} %get-tuple-element.78), channel_id=1, source_target_pairs={{8,16},{12,20},{16,8},{20,12},{9,17},{13,21},{17,9},{21,13}} | collective-permute-start | bytes 1179656 | tf_op jit(solution)/shard_map/cond/branch_1_fun/ppermute | solution.py:369
  15.9 4.9 %collective-permute-start.4 = (f16[2,3,16,2048]{3,2,1,0:T(8,128)(2,1)S(1)}, f16[2,3,16,2048]{3,2,1,0:T(8,128)(2,1)S(1)}, u32[]{:S(2)}, u32[]{:S(2)}) collective-permute-start(f16[2,3,16,2048]{3,2,1,0:T(8,128)(2,1)S(1)} %get-tuple-element.79), channel_id=1, source_target_pairs={{0,8},{4,12},{16,24},{20,28},{8,0},{12,4},{24,16},{28,20},{2,6},{6... | collective-permute-start | bytes 1179656 | tf_op jit(solution)/shard_map/cond/branch_1_fun/ppermute | solution.py:369
  21.0 0.6 %select_convert_fusion.1 = (f16[2,3,16,2048]{3,2,1,0:T(8,128)(2,1)S(1)}, f16[2,3,16,2048]{3,2,1,0:T(8,128)(2,1)S(1)}) fusion(f32[3,16,2048]{2,1,0:T(8,128)S(1)} %get-tuple-element.109, f32[3,16,2048]{2,1,0:T(8,128)S(1)} %get-tuple-element.108, f32[3,16,2048]{2,1,0:T(8,128)S(1)} %get-tuple-element.107, f32[3,16,2048]{2,1,0:T(8,128)S(1)} %get-tuple-element.106, ...), kind=kLoop, calls=%fused_computation.3 | loop fusion | flops 2752512 | bytes 3149844 | tf_op jit(solution)/shard_map/cond/branch_1_fun/convert_element_type | solution.py:487
  21.6 0.7 %collective-permute-start.9 = (f16[2,3,16,2048]{3,2,1,0:T(8,128)(2,1)S(1)}, f16[2,3,16,2048]{3,2,1,0:T(8,128)(2,1)S(1)}, u32[]{:S(2)}, u32[]{:S(2)}) collective-permute-start(f16[2,3,16,2048]{3,2,1,0:T(8,128)(2,1)S(1)} %get-tuple-element.76), channel_id=1, source_target_pairs={{8,16},{12,20},{16,8},{20,12},{9,17},{13,21},{17,9},{21,13}} | collective-permute-start | bytes 1179656 | tf_op jit(solution)/shard_map/cond/branch_1_fun/ppermute | solution.py:369
  22.4 0.6 %collective-permute-start.11 = (bf16[80,1024]{1,0:T(8,128)(2,1)S(1)}, bf16[80,1024]{1,0:T(8,128)(2,1)S(1)}, u32[]{:S(2)}, u32[]{:S(2)}) collective-permute-start(bf16[80,1024]{1,0:T(8,128)(2,1)S(1)} %slice_select_fusion), channel_id=1, source_target_pairs={{0,2},{2,0},{4,6},{6,4},{8,10},{10,8},{12,14},{14,12},{16,18},{18,... | collective-permute-start | bytes 491528 | tf_op jit(solution)/shard_map/cond/branch_1_fun/ppermute | solution.py:115
  23.1 2.2 %collective-permute-start.8 = (f16[2,3,16,2048]{3,2,1,0:T(8,128)(2,1)S(1)}, f16[2,3,16,2048]{3,2,1,0:T(8,128)(2,1)S(1)}, u32[]{:S(2)}, u32[]{:S(2)}) collective-permute-start(f16[2,3,16,2048]{3,2,1,0:T(8,128)(2,1)S(1)} %get-tuple-element.77), channel_id=1, source_target_pairs={{0,8},{4,12},{16,24},{20,28},{8,0},{12,4},{24,16},{28,20},{2,6},{6... | collective-permute-start | bytes 1179656 | tf_op jit(solution)/shard_map/cond/branch_1_fun/ppermute | solution.py:369
  25.4 2.1 %branch_1_fun.3.wind_ref = f32[2,2,80,2048]{3,2,1,0:T(8,128)S(1)} custom-call(s32[2]{0:T(128)S(1)} %pad_add_fusion.where_ref, bf16[160,1024]{1,0:T(8,128)(2,1)S(1)} %pad_maximum_fusion.coarse_ref), custom_call_target="tpu_custom_call" | custom-call | flops 52428800 | bytes 2621440 | tf_op jit(solution)/shard_map/cond/branch_1_fun/pallas_call | solution.py:147
  28.3 2.7 %collective-permute-done.8 = f16[2,3,16,2048]{3,2,1,0:T(8,128)(2,1)S(1)} collective-permute-done((f16[2,3,16,2048]{3,2,1,0:T(8,128)(2,1)S(1)}, f16[2,3,16,2048]{3,2,1,0:T(8,128)(2,1)S(1)}, u32[]{:S(2)}, u32[]{:S(2)}) %collective-permute-start.8) | collective-permute-done | bytes 393248 | tf_op jit(solution)/shard_map/cond/branch_1_fun/ppermute | solution.py:369
  31.9 1.2 %collective-permute-done.12 = f16[3,16,2048]{2,1,0:T(8,128)(2,1)S(1)} collective-permute-done((f16[3,16,2048]{2,1,0:T(8,128)(2,1)S(1)}, f16[3,16,2048]{2,1,0:T(8,128)(2,1)S(1)}, u32[]{:S(2)}, u32[]{:S(2)}) %collective-permute-start.12) | collective-permute-done | bytes 196640 | tf_op jit(solution)/shard_map/cond/branch_1_fun/ppermute | solution.py:369
  33.3 1.6 %collective-permute-start.13 = (f16[3,3,2048]{2,1,0:T(4,128)(2,1)S(1)}, f16[3,3,2048]{2,1,0:T(4,128)(2,1)S(1)}, u32[]{:S(2)}, u32[]{:S(2)}) collective-permute-start(f16[3,3,2048]{2,1,0:T(4,128)(2,1)S(1)} %slice_select_fusion.1), channel_id=1, source_target_pairs={{0,1},{1,0},{2,3},{3,2},{4,5},{5,4},{6,7},{7,6},{8,9},{9,8},{10,11... | collective-permute-start | bytes 110600 | tf_op jit(solution)/shard_map/cond/branch_1_fun/ppermute | solution.py:44
  35.2 3.5 %branch_1_fun.4.old_ref = f32[3,64,2048]{2,1,0:T(8,128)} custom-call(s32[1]{0:T(128)} %bitcast.15.where_ref, f32[3,64,2048]{2,1,0:T(8,128)S(1)} %maximum_convert_fusion.state_ref, f32[80,2048]{1,0:T(8,128)S(1)} %fusion.depth_ref, f32[2,2,80,2048]{3,2,1,0:T(8,128)S(1)} %branch_1_fun.3.wind_ref), custom_call_target="tpu_custom_call" | custom-call | flops 39321600 | bytes 6291456 | tf_op jit(solution)/shard_map/cond/branch_1_fun/pallas_call | solution.py:250
  38.9 2.1 %branch_1_fun.5 = f32[3,64,2048]{2,1,0:T(8,128)} custom-call(s32[1]{0:T(128)} %bitcast.15.where_ref, f32[3,16,2048]{2,1,0:T(8,128)S(1)} %fusion.10.above_ref, f32[3,16,2048]{2,1,0:T(8,128)S(1)} %fusion.8.below_ref, f32[80,2048]{1,0:T(8,128)S(1)} %fusion.depth_ref, f32[2,2,80,2048]{3,2,1,0:T(8,128)S(1)} %branch_1_fun.3.wind_ref, ...), custom_call_target="tpu_custom_call", output_to_operand_aliasing={{}: (5, {})} | custom-call | flops 9830400 | bytes 4915200 | tf_op jit(solution)/shard_map/cond/branch_1_fun/pallas_call | solution.py:312
  (73 shorter events, 4.1 us)
Async XLA Ops:
  3.7 1.9 %collective-permute-start = (f16[3,32,2048]{2,1,0:T(8,128)(2,1)S(1)}, f16[3,32,2048]{2,1,0:T(8,128)(2,1)S(1)}, u32[]{:S(2)}, u32[]{:S(2)}) collective-permute-start(f16[3,32,2048]{2,1,0:T(8,128)(2,1)S(1)} %get-tuple-element.45), channel_id=1, source_target_pairs={{0,2},{2,0},{4,6},{6,4},{8,10},{10,8},{12,14},{14,12},{16,18},{18,... | collective-permute-start | bytes 1179656 | tf_op jit(solution)/shard_map/cond/branch_1_fun/ppermute | solution.py:369
  5.1 5.3 %copy-start.4 = (s32[16]{0:T(128)S(1)}, s32[16]{0:T(128)}, u32[]{:S(2)}) copy-start(s32[16]{0:T(128)} %get-tuple-element.49) | copy-start | bytes 196 | tf_op jit(solution)/shard_map/cond
  5.6 5.6 %copy-start.1 = (f32[64,2048]{1,0:T(8,128)S(1)}, f32[64,2048]{1,0:T(8,128)}, u32[]{:S(2)}) copy-start(f32[64,2048]{1,0:T(8,128)} %get-tuple-element.54) | copy-start | bytes 1572868 | tf_op jit(solution)/shard_map/cond
  5.8 8.7 %collective-permute-start.2 = (f16[2,3,16,2048]{3,2,1,0:T(8,128)(2,1)S(1)}, f16[2,3,16,2048]{3,2,1,0:T(8,128)(2,1)S(1)}, u32[]{:S(2)}, u32[]{:S(2)}) collective-permute-start(f16[2,3,16,2048]{3,2,1,0:T(8,128)(2,1)S(1)} %get-tuple-element.50), channel_id=1, source_target_pairs={{0,4},{4,0},{8,12},{12,8},{16,20},{20,16},{24,28},{28,24},{2,10},{... | collective-permute-start | bytes 1179656 | tf_op jit(solution)/shard_map/cond/branch_1_fun/ppermute | solution.py:369
  8.8 5.9 %collective-permute-start.1 = (f16[2,3,16,2048]{3,2,1,0:T(8,128)(2,1)S(1)}, f16[2,3,16,2048]{3,2,1,0:T(8,128)(2,1)S(1)}, u32[]{:S(2)}, u32[]{:S(2)}) collective-permute-start(f16[2,3,16,2048]{3,2,1,0:T(8,128)(2,1)S(1)} %get-tuple-element.50), channel_id=1, source_target_pairs={{10,18},{14,22},{18,10},{22,14},{11,19},{15,23},{19,11},{23,15}} | collective-permute-start | bytes 1179656 | tf_op jit(solution)/shard_map/cond/branch_1_fun/ppermute | solution.py:369
  9.5 11.4 %collective-permute-start.6 = (f16[2,3,16,2048]{3,2,1,0:T(8,128)(2,1)S(1)}, f16[2,3,16,2048]{3,2,1,0:T(8,128)(2,1)S(1)}, u32[]{:S(2)}, u32[]{:S(2)}) collective-permute-start(f16[2,3,16,2048]{3,2,1,0:T(8,128)(2,1)S(1)} %get-tuple-element.51), channel_id=1, source_target_pairs={{10,18},{14,22},{18,10},{22,14},{11,19},{15,23},{19,11},{23,15}} | collective-permute-start | bytes 1179656 | tf_op jit(solution)/shard_map/cond/branch_1_fun/ppermute | solution.py:369
  10.3 10.6 %collective-permute-start.7 = (f16[2,3,16,2048]{3,2,1,0:T(8,128)(2,1)S(1)}, f16[2,3,16,2048]{3,2,1,0:T(8,128)(2,1)S(1)}, u32[]{:S(2)}, u32[]{:S(2)}) collective-permute-start(f16[2,3,16,2048]{3,2,1,0:T(8,128)(2,1)S(1)} %get-tuple-element.51), channel_id=1, source_target_pairs={{0,4},{4,0},{8,12},{12,8},{16,20},{20,16},{24,28},{28,24},{2,10},{... | collective-permute-start | bytes 1179656 | tf_op jit(solution)/shard_map/cond/branch_1_fun/ppermute | solution.py:369
  12.4 9.9 %collective-permute-start.10 = (bf16[92,1024]{1,0:T(8,128)(2,1)S(1)}, bf16[92,1024]{1,0:T(8,128)(2,1)S(1)}, u32[]{:S(2)}, u32[]{:S(2)}) collective-permute-start(bf16[92,1024]{1,0:T(8,128)(2,1)S(1)} %pad_maximum_fusion.1), channel_id=1, source_target_pairs={{0,1},{1,0},{2,3},{3,2},{4,5},{5,4},{6,7},{7,6},{8,9},{9,8},{10,11... | collective-permute-start | bytes 565256 | tf_op jit(solution)/shard_map/cond/branch_1_fun/ppermute | solution.py:90
  15.2 12.4 %collective-permute-start.3 = (f16[2,3,16,2048]{3,2,1,0:T(8,128)(2,1)S(1)}, f16[2,3,16,2048]{3,2,1,0:T(8,128)(2,1)S(1)}, u32[]{:S(2)}, u32[]{:S(2)}) collective-permute-start(f16[2,3,16,2048]{3,2,1,0:T(8,128)(2,1)S(1)} %get-tuple-element.78), channel_id=1, source_target_pairs={{8,16},{12,20},{16,8},{20,12},{9,17},{13,21},{17,9},{21,13}} | collective-permute-start | bytes 1179656 | tf_op jit(solution)/shard_map/cond/branch_1_fun/ppermute | solution.py:369
  15.9 11.8 %collective-permute-start.4 = (f16[2,3,16,2048]{3,2,1,0:T(8,128)(2,1)S(1)}, f16[2,3,16,2048]{3,2,1,0:T(8,128)(2,1)S(1)}, u32[]{:S(2)}, u32[]{:S(2)}) collective-permute-start(f16[2,3,16,2048]{3,2,1,0:T(8,128)(2,1)S(1)} %get-tuple-element.79), channel_id=1, source_target_pairs={{0,8},{4,12},{16,24},{20,28},{8,0},{12,4},{24,16},{28,20},{2,6},{6... | collective-permute-start | bytes 1179656 | tf_op jit(solution)/shard_map/cond/branch_1_fun/ppermute | solution.py:369
  21.6 9.4 %collective-permute-start.9 = (f16[2,3,16,2048]{3,2,1,0:T(8,128)(2,1)S(1)}, f16[2,3,16,2048]{3,2,1,0:T(8,128)(2,1)S(1)}, u32[]{:S(2)}, u32[]{:S(2)}) collective-permute-start(f16[2,3,16,2048]{3,2,1,0:T(8,128)(2,1)S(1)} %get-tuple-element.76), channel_id=1, source_target_pairs={{8,16},{12,20},{16,8},{20,12},{9,17},{13,21},{17,9},{21,13}} | collective-permute-start | bytes 1179656 | tf_op jit(solution)/shard_map/cond/branch_1_fun/ppermute | solution.py:369
  22.4 2.9 %collective-permute-start.11 = (bf16[80,1024]{1,0:T(8,128)(2,1)S(1)}, bf16[80,1024]{1,0:T(8,128)(2,1)S(1)}, u32[]{:S(2)}, u32[]{:S(2)}) collective-permute-start(bf16[80,1024]{1,0:T(8,128)(2,1)S(1)} %slice_select_fusion), channel_id=1, source_target_pairs={{0,2},{2,0},{4,6},{6,4},{8,10},{10,8},{12,14},{14,12},{16,18},{18,... | collective-permute-start | bytes 491528 | tf_op jit(solution)/shard_map/cond/branch_1_fun/ppermute | solution.py:115
  23.1 7.9 %collective-permute-start.8 = (f16[2,3,16,2048]{3,2,1,0:T(8,128)(2,1)S(1)}, f16[2,3,16,2048]{3,2,1,0:T(8,128)(2,1)S(1)}, u32[]{:S(2)}, u32[]{:S(2)}) collective-permute-start(f16[2,3,16,2048]{3,2,1,0:T(8,128)(2,1)S(1)} %get-tuple-element.77), channel_id=1, source_target_pairs={{0,8},{4,12},{16,24},{20,28},{8,0},{12,4},{24,16},{28,20},{2,6},{6... | collective-permute-start | bytes 1179656 | tf_op jit(solution)/shard_map/cond/branch_1_fun/ppermute | solution.py:369
  28.2 3.6 %collective-permute-start.5 = (f16[3,16,2048]{2,1,0:T(8,128)(2,1)S(1)}, f16[3,16,2048]{2,1,0:T(8,128)(2,1)S(1)}, u32[]{:S(2)}, u32[]{:S(2)}) collective-permute-start(f16[3,16,2048]{2,1,0:T(8,128)(2,1)S(1)} %slice_bitcast_fusion.7), channel_id=1, source_target_pairs={{0,2},{2,0},{4,6},{6,4},{8,10},{10,8},{12,14},{14,12},{16,18},{18,... | collective-permute-start | bytes 589832 | tf_op jit(solution)/shard_map/cond/branch_1_fun/ppermute | solution.py:369
  31.6 1.5 %collective-permute-start.12 = (f16[3,16,2048]{2,1,0:T(8,128)(2,1)S(1)}, f16[3,16,2048]{2,1,0:T(8,128)(2,1)S(1)}, u32[]{:S(2)}, u32[]{:S(2)}) collective-permute-start(f16[3,16,2048]{2,1,0:T(8,128)(2,1)S(1)} %slice_bitcast_fusion), channel_id=1, source_target_pairs={{0,2},{2,0},{4,6},{6,4},{8,10},{10,8},{12,14},{14,12},{16,18},{18,... | collective-permute-start | bytes 589832 | tf_op jit(solution)/shard_map/cond/branch_1_fun/ppermute | solution.py:369
  33.3 5.4 %collective-permute-start.13 = (f16[3,3,2048]{2,1,0:T(4,128)(2,1)S(1)}, f16[3,3,2048]{2,1,0:T(4,128)(2,1)S(1)}, u32[]{:S(2)}, u32[]{:S(2)}) collective-permute-start(f16[3,3,2048]{2,1,0:T(4,128)(2,1)S(1)} %slice_select_fusion.1), channel_id=1, source_target_pairs={{0,1},{1,0},{2,3},{3,2},{4,5},{5,4},{6,7},{7,6},{8,9},{9,8},{10,11... | collective-permute-start | bytes 110600 | tf_op jit(solution)/shard_map/cond/branch_1_fun/ppermute | solution.py:44

commit v2 on v1

--- a/solution.py
+++ b/solution.py
@@ -1,4 +1,5 @@
 import functools
+import math
 
 import jax
 import jax.numpy as jnp
@@ -333,9 +334,21 @@
 
 
 def exchange_all(cells, parents):
-    spread = lax.all_to_all(cells[None], "dom", split_axis=3, concat_axis=0, tiled=True)
+    count = lax.axis_size("dom")
+    parts, rows, cols = cells.shape
+    tall = math.gcd(count, rows // PAD)
+    broad = count // tall
+    height, width = rows // tall, cols // broad
+    shares = cells.reshape(parts, tall, height, broad, width).transpose(1, 3, 0, 2, 4)
+    shares = shares.reshape(count, parts, height, width).astype(jnp.float16)
+    spread = lax.all_to_all(shares, "dom", split_axis=0, concat_axis=0, tiled=True)
     picked = jnp.take(spread, parents, axis=0, mode="clip")
-    return lax.all_to_all(picked, "dom", split_axis=0, concat_axis=3, tiled=True)[0]
+    back = lax.all_to_all(picked, "dom", split_axis=0, concat_axis=0, tiled=True)
+    lines = [
+        jnp.concatenate([back[row * broad + col] for col in range(broad)], axis=2)
+        for row in range(tall)
+    ]
+    return jnp.concatenate(lines, axis=1)
 
 
 def wide(array):
@@ -460,7 +473,7 @@
     def far():
         around = surroundings(sea_depth, wind, start_hour)
         parents = parents_by_starts(offspring)(slots)
-        copied = exchange_all(state.astype(jnp.float16), parents)
+        copied = exchange_all(state, parents)
         return finish([copied], *fields(around))
 
     def near():

time: 41.6 us -> 42.3 us (1.017)
  waiting for transfers between devices: 4.42 us -> 5.28 us
    ppermute x11, waiting for transfers between devices: 4.42 us -> 5.27 us  [move(): return lax.ppermute(array, 'dom', pairs) if pairs else array]
    ppermute x1, starting transfers between devices: 0.64 us -> 0.07 us  [assembled(): other = lax.ppermute(found, 'dom', [(i, i ^ 1) for i in range(devices)])]
    ppermute x11, starting transfers between devices: 13.8 us -> 14.4 us  [move(): return lax.ppermute(array, 'dom', pairs) if pairs else array]
  transfers between devices with their start and end apart: 14 -> 14, of which waited for: 3 -> 4; matrix products, arithmetic and copies ran while one was open for 13% -> 13% of each run, Pallas kernels for 14% -> 13%
where the time goes in v2:
time: 42.3 us; the launch traced here: 42 us
  starting transfers between devices  18 us (43%)
  Pallas kernels  7.5 us (18%)
  other arithmetic  7.44 us (18%)
  waiting for transfers between devices  5.28 us (12%)
  loops' own time  1.51 us (4%)
  local copies, waits for them, and re-layouts  1.4 us (3%)
  between operations  0.85 us (2%)
    ppermute x11, starting transfers between devices, move(): return lax.ppermute(array, 'dom', pairs) if pairs else array  14.4 us
    ppermute x11, waiting for transfers between devices, move(): return lax.ppermute(array, 'dom', pairs) if pairs else array  5.27 us
    pallas_call x1, Pallas kernels, step(): pl.pallas_call(functools.partial(step_kernel, total_rows), out_shape=jax....  3.32 us
    pallas_call x1, Pallas kernels, fine_wind(): pl.pallas_call(wind_kernel, out_shape=jax.ShapeDtypeStruct((hours, parts,...  2.13 us
    pallas_call x1, Pallas kernels, mend(): pl.pallas_call(functools.partial(edge_kernel, total_rows), out_shape=jax....  2.06 us
    ppermute x1, starting transfers between devices, surroundings(): sent.append(lax.ppermute(message, 'tile', pairs))  2.03 us
    ppermute x1, starting transfers between devices, swap_edges(): got = lax.ppermute(jnp.where(upper, tail, head), 'tile', pairs)  1.56 us
    another operation x1, loops' own time, body(): return lax.cond(close, near, far)[None]  1.51 us
  transfers between devices with their start and end apart: 14, of which 4 were waited for; matrix products, arithmetic and copies ran while one was open for 13% of the time, Pallas kernels for 13%

profile of v2, /device:TPU:0, one launch (start us, length us, event | category | flops | bytes accessed | tf_op | source)
XLA Modules:
  0.0 42.0 jit_solution(4288738672894861528)
XLA Ops:
  0.0 0.8 %select_reduce_fusion.1 = s32[4]{0:T(128)S(1)} fusion(s32[16]{0:T(128)} %param.8, s32[4]{0:T(128)S(1)} %add_multiply_fusion), kind=kLoop, calls=%fused_computation.264 | loop fusion | flops 188 | bytes 96 | tf_op jit(solution)/shard_map/reduce_sum | solution.py:515
  0.8 0.6 %compare_reduce_fusion.3 = pred[]{:T(512)} fusion(s32[4]{0:T(128)S(1)} %select_reduce_fusion.1, s32[16]{0:T(128)S(1)} %iota.43), kind=kLoop, calls=%fused_computation.266 | loop fusion | flops 23 | bytes 33 | tf_op jit(solution)/shard_map/reduce_and | solution.py:516
  2.2 39.7 %conditional.1 = (f32[1,3,64,2048]{3,2,1,0:T(8,128)}) conditional(s32[]{:T(128)} %convert_element_type.232, (s32[]{:T(128)}, f32[1,3,64,2048]{3,2,1,0:T(8,128)}, s32[16]{0:T(128)}, s32[16]{0:T(128)S(1)}, s32[1]{0:T(128)}, /*index=5*/bf16[3,2,64,1024]{3,2,1,0:T(8,128)(2,1)}, f32[64,2048]{1,0:T(8,128)}) %tuple.16, (s32[]{:T(128)}, ...), branch_computations={%region_2.5_spmd, %region_5.10_spmd} | conditional | flops 120164016 | bytes 79011016 | solution.py:517
  2.2 1.5 %fusion.5 = (f16[3,32,2048]{2,1,0:T(8,128)(2,1)S(1)}, f32[3,32,2048]{2,1,0:T(8,128)S(1)}) fusion(f32[1,3,64,2048]{3,2,1,0:T(8,128)} %get-tuple-element.44, s32[]{:T(128)S(6)} %select_n.421, s32[]{:T(128)S(6)} %select_n.420), kind=kLoop, calls=%fused_computation.25 | loop fusion | flops 196608 | bytes 2752520 | tf_op jit(solution)/shard_map/cond/branch_1_fun/convert_element_type | solution.py:402
  3.7 0.5 %collective-permute-start = (f16[3,32,2048]{2,1,0:T(8,128)(2,1)S(1)}, f16[3,32,2048]{2,1,0:T(8,128)(2,1)S(1)}, u32[]{:S(2)}, u32[]{:S(2)}) collective-permute-start(f16[3,32,2048]{2,1,0:T(8,128)(2,1)S(1)} %get-tuple-element.46), channel_id=1, source_target_pairs={{0,2},{2,0},{4,6},{6,4},{8,10},{10,8},{12,14},{14,12},{16,18},{18,... | collective-permute-start | bytes 1179656 | tf_op jit(solution)/shard_map/cond/branch_1_fun/ppermute | solution.py:382
  5.9 0.7 %collective-permute-start.1 = (f16[2,3,16,2048]{3,2,1,0:T(8,128)(2,1)S(1)}, f16[2,3,16,2048]{3,2,1,0:T(8,128)(2,1)S(1)}, u32[]{:S(2)}, u32[]{:S(2)}) collective-permute-start(f16[2,3,16,2048]{3,2,1,0:T(8,128)(2,1)S(1)} %get-tuple-element.51), channel_id=1, source_target_pairs={{10,18},{14,22},{18,10},{22,14},{11,19},{15,23},{19,11},{23,15}} | collective-permute-start | bytes 1179656 | tf_op jit(solution)/shard_map/cond/branch_1_fun/ppermute | solution.py:382
  6.5 3.0 %collective-permute-start.2 = (f16[2,3,16,2048]{3,2,1,0:T(8,128)(2,1)S(1)}, f16[2,3,16,2048]{3,2,1,0:T(8,128)(2,1)S(1)}, u32[]{:S(2)}, u32[]{:S(2)}) collective-permute-start(f16[2,3,16,2048]{3,2,1,0:T(8,128)(2,1)S(1)} %get-tuple-element.51), channel_id=1, source_target_pairs={{0,4},{4,0},{8,12},{12,8},{16,20},{20,16},{24,28},{28,24},{2,10},{... | collective-permute-start | bytes 1179656 | tf_op jit(solution)/shard_map/cond/branch_1_fun/ppermute | solution.py:382
  9.5 0.7 %collective-permute-start.6 = (f16[2,3,16,2048]{3,2,1,0:T(8,128)(2,1)S(1)}, f16[2,3,16,2048]{3,2,1,0:T(8,128)(2,1)S(1)}, u32[]{:S(2)}, u32[]{:S(2)}) collective-permute-start(f16[2,3,16,2048]{3,2,1,0:T(8,128)(2,1)S(1)} %get-tuple-element.52), channel_id=1, source_target_pairs={{10,18},{14,22},{18,10},{22,14},{11,19},{15,23},{19,11},{23,15}} | collective-permute-start | bytes 1179656 | tf_op jit(solution)/shard_map/cond/branch_1_fun/ppermute | solution.py:382
  11.1 1.1 %constant_dynamic-slice_fusion = (bf16[1,2,40,1024]{3,2,1,0:T(8,128)(2,1)S(1)}, bf16[1,2,40,1024]{3,2,1,0:T(8,128)(2,1)S(1)}) fusion(bf16[3,2,64,1024]{3,2,1,0:T(8,128)(2,1)} %get-tuple-element.53, s32[]{:T(128)S(6)} %select_n.497, s32[]{:T(128)} %min.24, s32[]{:T(128)S(6)} %min.23), kind=kLoop, calls=%fused_computation.131 | loop fusion | bytes 655372 | tf_op jit(solution)/shard_map/cond/branch_1_fun/dynamic_slice | solution.py:79
  12.2 2.0 %collective-permute-start.10 = (bf16[92,1024]{1,0:T(8,128)(2,1)S(1)}, bf16[92,1024]{1,0:T(8,128)(2,1)S(1)}, u32[]{:S(2)}, u32[]{:S(2)}) collective-permute-start(bf16[92,1024]{1,0:T(8,128)(2,1)S(1)} %pad_maximum_fusion.1), channel_id=1, source_target_pairs={{0,1},{1,0},{2,3},{3,2},{4,5},{5,4},{6,7},{7,6},{8,9},{9,8},{10,11... | collective-permute-start | bytes 565256 | tf_op jit(solution)/shard_map/cond/branch_1_fun/ppermute | solution.py:91
  14.5 0.8 %collective-permute-done.2 = f16[2,3,16,2048]{3,2,1,0:T(8,128)(2,1)S(1)} collective-permute-done((f16[2,3,16,2048]{3,2,1,0:T(8,128)(2,1)S(1)}, f16[2,3,16,2048]{3,2,1,0:T(8,128)(2,1)S(1)}, u32[]{:S(2)}, u32[]{:S(2)}) %collective-permute-start.2) | collective-permute-done | bytes 393248 | tf_op jit(solution)/shard_map/cond/branch_1_fun/ppermute | solution.py:382
  15.3 0.5 %select_convert_fusion.5 = (f16[2,3,16,2048]{3,2,1,0:T(8,128)(2,1)S(1)}, f16[2,3,16,2048]{3,2,1,0:T(8,128)(2,1)S(1)}) fusion(f32[3,16,2048]{2,1,0:T(8,128)S(1)} %get-tuple-element.90, f32[3,16,2048]{2,1,0:T(8,128)S(1)} %get-tuple-element.89, f32[3,16,2048]{2,1,0:T(8,128)S(1)} %get-tuple-element.88, f32[3,16,2048]{2,1,0:T(8,128)S(1)} %get-tuple-element.87, ...), kind=kLoop, calls=%fused_computation.7 | loop fusion | flops 2359296 | bytes 3145748 | tf_op jit(solution)/shard_map/cond/branch_1_fun/convert_element_type | solution.py:500
  15.8 0.7 %collective-permute-start.3 = (f16[2,3,16,2048]{3,2,1,0:T(8,128)(2,1)S(1)}, f16[2,3,16,2048]{3,2,1,0:T(8,128)(2,1)S(1)}, u32[]{:S(2)}, u32[]{:S(2)}) collective-permute-start(f16[2,3,16,2048]{3,2,1,0:T(8,128)(2,1)S(1)} %get-tuple-element.65), channel_id=1, source_target_pairs={{8,16},{12,20},{16,8},{20,12},{9,17},{13,21},{17,9},{21,13}} | collective-permute-start | bytes 1179656 | tf_op jit(solution)/shard_map/cond/branch_1_fun/ppermute | solution.py:382
  16.5 4.9 %collective-permute-start.4 = (f16[2,3,16,2048]{3,2,1,0:T(8,128)(2,1)S(1)}, f16[2,3,16,2048]{3,2,1,0:T(8,128)(2,1)S(1)}, u32[]{:S(2)}, u32[]{:S(2)}) collective-permute-start(f16[2,3,16,2048]{3,2,1,0:T(8,128)(2,1)S(1)} %get-tuple-element.66), channel_id=1, source_target_pairs={{0,8},{4,12},{16,24},{20,28},{8,0},{12,4},{24,16},{28,20},{2,6},{6... | collective-permute-start | bytes 1179656 | tf_op jit(solution)/shard_map/cond/branch_1_fun/ppermute | solution.py:382
  21.7 0.6 %select_convert_fusion.1 = (f16[2,3,16,2048]{3,2,1,0:T(8,128)(2,1)S(1)}, f16[2,3,16,2048]{3,2,1,0:T(8,128)(2,1)S(1)}) fusion(f32[3,16,2048]{2,1,0:T(8,128)S(1)} %get-tuple-element.96, f32[3,16,2048]{2,1,0:T(8,128)S(1)} %get-tuple-element.95, f32[3,16,2048]{2,1,0:T(8,128)S(1)} %get-tuple-element.94, f32[3,16,2048]{2,1,0:T(8,128)S(1)} %get-tuple-element.93, ...), kind=kLoop, calls=%fused_computation.3 | loop fusion | flops 2752512 | bytes 3149844 | tf_op jit(solution)/shard_map/cond/branch_1_fun/convert_element_type | solution.py:500
  22.2 0.9 %collective-permute-start.9 = (f16[2,3,16,2048]{3,2,1,0:T(8,128)(2,1)S(1)}, f16[2,3,16,2048]{3,2,1,0:T(8,128)(2,1)S(1)}, u32[]{:S(2)}, u32[]{:S(2)}) collective-permute-start(f16[2,3,16,2048]{3,2,1,0:T(8,128)(2,1)S(1)} %get-tuple-element.63), channel_id=1, source_target_pairs={{8,16},{12,20},{16,8},{20,12},{9,17},{13,21},{17,9},{21,13}} | collective-permute-start | bytes 1179656 | tf_op jit(solution)/shard_map/cond/branch_1_fun/ppermute | solution.py:382
  23.3 2.8 %collective-permute-start.8 = (f16[2,3,16,2048]{3,2,1,0:T(8,128)(2,1)S(1)}, f16[2,3,16,2048]{3,2,1,0:T(8,128)(2,1)S(1)}, u32[]{:S(2)}, u32[]{:S(2)}) collective-permute-start(f16[2,3,16,2048]{3,2,1,0:T(8,128)(2,1)S(1)} %get-tuple-element.64), channel_id=1, source_target_pairs={{0,8},{4,12},{16,24},{20,28},{8,0},{12,4},{24,16},{28,20},{2,6},{6... | collective-permute-start | bytes 1179656 | tf_op jit(solution)/shard_map/cond/branch_1_fun/ppermute | solution.py:382
  26.3 2.1 %branch_1_fun.3.wind_ref = f32[2,2,80,2048]{3,2,1,0:T(8,128)S(1)} custom-call(s32[2]{0:T(128)S(1)} %pad_add_fusion.where_ref, bf16[160,1024]{1,0:T(8,128)(2,1)S(1)} %pad_maximum_fusion.coarse_ref), custom_call_target="tpu_custom_call" | custom-call | flops 52428800 | bytes 2621440 | tf_op jit(solution)/shard_map/cond/branch_1_fun/pallas_call | solution.py:148
  29.2 2.7 %collective-permute-done.8 = f16[2,3,16,2048]{3,2,1,0:T(8,128)(2,1)S(1)} collective-permute-done((f16[2,3,16,2048]{3,2,1,0:T(8,128)(2,1)S(1)}, f16[2,3,16,2048]{3,2,1,0:T(8,128)(2,1)S(1)}, u32[]{:S(2)}, u32[]{:S(2)}) %collective-permute-start.8) | collective-permute-done | bytes 393248 | tf_op jit(solution)/shard_map/cond/branch_1_fun/ppermute | solution.py:382
  32.0 0.5 %select_convert_fusion = f16[2,3,16,2048]{3,2,1,0:T(8,128)(2,1)S(1)} fusion(f32[3,16,2048]{2,1,0:T(8,128)S(1)} %get-tuple-element.84, f32[3,16,2048]{2,1,0:T(8,128)S(1)} %get-tuple-element.83, f32[3,16,2048]{2,1,0:T(8,128)S(1)} %get-tuple-element.82, f32[3,16,2048]{2,1,0:T(8,128)S(1)} %get-tuple-element.81, f32[3,16,2048]{2,1,0:T(8,128)S(1)} %get-tuple-element.96, ...), kind=kLoop, calls=%fused_computation.2 | loop fusion | flops 1966080 | bytes 4325394 | tf_op jit(solution)/shard_map/cond/branch_1_fun/convert_element_type | solution.py:443
  32.7 1.3 %collective-permute-done.12 = f16[3,16,2048]{2,1,0:T(8,128)(2,1)S(1)} collective-permute-done((f16[3,16,2048]{2,1,0:T(8,128)(2,1)S(1)}, f16[3,16,2048]{2,1,0:T(8,128)(2,1)S(1)}, u32[]{:S(2)}, u32[]{:S(2)}) %collective-permute-start.12) | collective-permute-done | bytes 196640 | tf_op jit(solution)/shard_map/cond/branch_1_fun/ppermute | solution.py:382
  34.2 1.6 %collective-permute-start.13 = (f16[3,3,2048]{2,1,0:T(4,128)(2,1)S(1)}, f16[3,3,2048]{2,1,0:T(4,128)(2,1)S(1)}, u32[]{:S(2)}, u32[]{:S(2)}) collective-permute-start(f16[3,3,2048]{2,1,0:T(4,128)(2,1)S(1)} %slice_select_fusion.1), channel_id=1, source_target_pairs={{0,1},{1,0},{2,3},{3,2},{4,5},{5,4},{6,7},{7,6},{8,9},{9,8},{10,11... | collective-permute-start | bytes 110600 | tf_op jit(solution)/shard_map/cond/branch_1_fun/ppermute | solution.py:45
  36.1 3.3 %branch_1_fun.4.old_ref = f32[3,64,2048]{2,1,0:T(8,128)} custom-call(s32[1]{0:T(128)} %bitcast.27.where_ref, f32[3,64,2048]{2,1,0:T(8,128)S(1)} %maximum_convert_fusion.state_ref, f32[80,2048]{1,0:T(8,128)S(1)} %fusion.depth_ref, f32[2,2,80,2048]{3,2,1,0:T(8,128)S(1)} %branch_1_fun.3.wind_ref), custom_call_target="tpu_custom_call" | custom-call | flops 39321600 | bytes 6291456 | tf_op jit(solution)/shard_map/cond/branch_1_fun/pallas_call | solution.py:251
  39.6 2.1 %branch_1_fun.5 = f32[3,64,2048]{2,1,0:T(8,128)} custom-call(s32[1]{0:T(128)} %bitcast.27.where_ref, f32[3,16,2048]{2,1,0:T(8,128)S(1)} %fusion.11.above_ref, f32[3,16,2048]{2,1,0:T(8,128)S(1)} %fusion.9.below_ref, f32[80,2048]{1,0:T(8,128)S(1)} %fusion.depth_ref, f32[2,2,80,2048]{3,2,1,0:T(8,128)S(1)} %branch_1_fun.3.wind_ref, ...), custom_call_target="tpu_custom_call", output_to_operand_aliasing={{}: (5, {})} | custom-call | flops 9830400 | bytes 4915200 | tf_op jit(solution)/shard_map/cond/branch_1_fun/pallas_call | solution.py:313
  (73 shorter events, 4.0 us)
Async XLA Ops:
  3.7 1.9 %collective-permute-start = (f16[3,32,2048]{2,1,0:T(8,128)(2,1)S(1)}, f16[3,32,2048]{2,1,0:T(8,128)(2,1)S(1)}, u32[]{:S(2)}, u32[]{:S(2)}) collective-permute-start(f16[3,32,2048]{2,1,0:T(8,128)(2,1)S(1)} %get-tuple-element.46), channel_id=1, source_target_pairs={{0,2},{2,0},{4,6},{6,4},{8,10},{10,8},{12,14},{14,12},{16,18},{18,... | collective-permute-start | bytes 1179656 | tf_op jit(solution)/shard_map/cond/branch_1_fun/ppermute | solution.py:382
  5.1 5.2 %copy-start.3 = (s32[16]{0:T(128)S(1)}, s32[16]{0:T(128)}, u32[]{:S(2)}) copy-start(s32[16]{0:T(128)} %get-tuple-element.50) | copy-start | bytes 196 | tf_op jit(solution)/shard_map/cond
  5.6 5.4 %copy-start.1 = (f32[64,2048]{1,0:T(8,128)S(1)}, f32[64,2048]{1,0:T(8,128)}, u32[]{:S(2)}) copy-start(f32[64,2048]{1,0:T(8,128)} %get-tuple-element.55) | copy-start | bytes 1572868 | tf_op jit(solution)/shard_map/cond
  5.9 8.6 %collective-permute-start.1 = (f16[2,3,16,2048]{3,2,1,0:T(8,128)(2,1)S(1)}, f16[2,3,16,2048]{3,2,1,0:T(8,128)(2,1)S(1)}, u32[]{:S(2)}, u32[]{:S(2)}) collective-permute-start(f16[2,3,16,2048]{3,2,1,0:T(8,128)(2,1)S(1)} %get-tuple-element.51), channel_id=1, source_target_pairs={{10,18},{14,22},{18,10},{22,14},{11,19},{15,23},{19,11},{23,15}} | collective-permute-start | bytes 1179656 | tf_op jit(solution)/shard_map/cond/branch_1_fun/ppermute | solution.py:382
  6.5 8.7 %collective-permute-start.2 = (f16[2,3,16,2048]{3,2,1,0:T(8,128)(2,1)S(1)}, f16[2,3,16,2048]{3,2,1,0:T(8,128)(2,1)S(1)}, u32[]{:S(2)}, u32[]{:S(2)}) collective-permute-start(f16[2,3,16,2048]{3,2,1,0:T(8,128)(2,1)S(1)} %get-tuple-element.51), channel_id=1, source_target_pairs={{0,4},{4,0},{8,12},{12,8},{16,20},{20,16},{24,28},{28,24},{2,10},{... | collective-permute-start | bytes 1179656 | tf_op jit(solution)/shard_map/cond/branch_1_fun/ppermute | solution.py:382
  9.5 12.0 %collective-permute-start.6 = (f16[2,3,16,2048]{3,2,1,0:T(8,128)(2,1)S(1)}, f16[2,3,16,2048]{3,2,1,0:T(8,128)(2,1)S(1)}, u32[]{:S(2)}, u32[]{:S(2)}) collective-permute-start(f16[2,3,16,2048]{3,2,1,0:T(8,128)(2,1)S(1)} %get-tuple-element.52), channel_id=1, source_target_pairs={{10,18},{14,22},{18,10},{22,14},{11,19},{15,23},{19,11},{23,15}} | collective-permute-start | bytes 1179656 | tf_op jit(solution)/shard_map/cond/branch_1_fun/ppermute | solution.py:382
  10.2 11.4 %collective-permute-start.7 = (f16[2,3,16,2048]{3,2,1,0:T(8,128)(2,1)S(1)}, f16[2,3,16,2048]{3,2,1,0:T(8,128)(2,1)S(1)}, u32[]{:S(2)}, u32[]{:S(2)}) collective-permute-start(f16[2,3,16,2048]{3,2,1,0:T(8,128)(2,1)S(1)} %get-tuple-element.52), channel_id=1, source_target_pairs={{0,4},{4,0},{8,12},{12,8},{16,20},{20,16},{24,28},{28,24},{2,10},{... | collective-permute-start | bytes 1179656 | tf_op jit(solution)/shard_map/cond/branch_1_fun/ppermute | solution.py:382
  12.2 10.9 %collective-permute-start.10 = (bf16[92,1024]{1,0:T(8,128)(2,1)S(1)}, bf16[92,1024]{1,0:T(8,128)(2,1)S(1)}, u32[]{:S(2)}, u32[]{:S(2)}) collective-permute-start(bf16[92,1024]{1,0:T(8,128)(2,1)S(1)} %pad_maximum_fusion.1), channel_id=1, source_target_pairs={{0,1},{1,0},{2,3},{3,2},{4,5},{5,4},{6,7},{7,6},{8,9},{9,8},{10,11... | collective-permute-start | bytes 565256 | tf_op jit(solution)/shard_map/cond/branch_1_fun/ppermute | solution.py:91
  15.8 12.7 %collective-permute-start.3 = (f16[2,3,16,2048]{3,2,1,0:T(8,128)(2,1)S(1)}, f16[2,3,16,2048]{3,2,1,0:T(8,128)(2,1)S(1)}, u32[]{:S(2)}, u32[]{:S(2)}) collective-permute-start(f16[2,3,16,2048]{3,2,1,0:T(8,128)(2,1)S(1)} %get-tuple-element.65), channel_id=1, source_target_pairs={{8,16},{12,20},{16,8},{20,12},{9,17},{13,21},{17,9},{21,13}} | collective-permute-start | bytes 1179656 | tf_op jit(solution)/shard_map/cond/branch_1_fun/ppermute | solution.py:382
  16.5 12.1 %collective-permute-start.4 = (f16[2,3,16,2048]{3,2,1,0:T(8,128)(2,1)S(1)}, f16[2,3,16,2048]{3,2,1,0:T(8,128)(2,1)S(1)}, u32[]{:S(2)}, u32[]{:S(2)}) collective-permute-start(f16[2,3,16,2048]{3,2,1,0:T(8,128)(2,1)S(1)} %get-tuple-element.66), channel_id=1, source_target_pairs={{0,8},{4,12},{16,24},{20,28},{8,0},{12,4},{24,16},{28,20},{2,6},{6... | collective-permute-start | bytes 1179656 | tf_op jit(solution)/shard_map/cond/branch_1_fun/ppermute | solution.py:382
  22.2 9.7 %collective-permute-start.9 = (f16[2,3,16,2048]{3,2,1,0:T(8,128)(2,1)S(1)}, f16[2,3,16,2048]{3,2,1,0:T(8,128)(2,1)S(1)}, u32[]{:S(2)}, u32[]{:S(2)}) collective-permute-start(f16[2,3,16,2048]{3,2,1,0:T(8,128)(2,1)S(1)} %get-tuple-element.63), channel_id=1, source_target_pairs={{8,16},{12,20},{16,8},{20,12},{9,17},{13,21},{17,9},{21,13}} | collective-permute-start | bytes 1179656 | tf_op jit(solution)/shard_map/cond/branch_1_fun/ppermute | solution.py:382
  23.2 3.0 %collective-permute-start.11 = (bf16[80,1024]{1,0:T(8,128)(2,1)S(1)}, bf16[80,1024]{1,0:T(8,128)(2,1)S(1)}, u32[]{:S(2)}, u32[]{:S(2)}) collective-permute-start(bf16[80,1024]{1,0:T(8,128)(2,1)S(1)} %slice_select_fusion), channel_id=1, source_target_pairs={{0,2},{2,0},{4,6},{6,4},{8,10},{10,8},{12,14},{14,12},{16,18},{18,... | collective-permute-start | bytes 491528 | tf_op jit(solution)/shard_map/cond/branch_1_fun/ppermute | solution.py:116
  23.3 8.6 %collective-permute-start.8 = (f16[2,3,16,2048]{3,2,1,0:T(8,128)(2,1)S(1)}, f16[2,3,16,2048]{3,2,1,0:T(8,128)(2,1)S(1)}, u32[]{:S(2)}, u32[]{:S(2)}) collective-permute-start(f16[2,3,16,2048]{3,2,1,0:T(8,128)(2,1)S(1)} %get-tuple-element.64), channel_id=1, source_target_pairs={{0,8},{4,12},{16,24},{20,28},{8,0},{12,4},{24,16},{28,20},{2,6},{6... | collective-permute-start | bytes 1179656 | tf_op jit(solution)/shard_map/cond/branch_1_fun/ppermute | solution.py:382
  29.1 3.5 %collective-permute-start.5 = (f16[3,16,2048]{2,1,0:T(8,128)(2,1)S(1)}, f16[3,16,2048]{2,1,0:T(8,128)(2,1)S(1)}, u32[]{:S(2)}, u32[]{:S(2)}) collective-permute-start(f16[3,16,2048]{2,1,0:T(8,128)(2,1)S(1)} %slice_bitcast_fusion.7), channel_id=1, source_target_pairs={{0,2},{2,0},{4,6},{6,4},{8,10},{10,8},{12,14},{14,12},{16,18},{18,... | collective-permute-start | bytes 589832 | tf_op jit(solution)/shard_map/cond/branch_1_fun/ppermute | solution.py:382
  32.5 1.5 %collective-permute-start.12 = (f16[3,16,2048]{2,1,0:T(8,128)(2,1)S(1)}, f16[3,16,2048]{2,1,0:T(8,128)(2,1)S(1)}, u32[]{:S(2)}, u32[]{:S(2)}) collective-permute-start(f16[3,16,2048]{2,1,0:T(8,128)(2,1)S(1)} %slice_bitcast_fusion), channel_id=1, source_target_pairs={{0,2},{2,0},{4,6},{6,4},{8,10},{10,8},{12,14},{14,12},{16,18},{18,... | collective-permute-start | bytes 589832 | tf_op jit(solution)/shard_map/cond/branch_1_fun/ppermute | solution.py:382
  34.2 5.2 %collective-permute-start.13 = (f16[3,3,2048]{2,1,0:T(4,128)(2,1)S(1)}, f16[3,3,2048]{2,1,0:T(4,128)(2,1)S(1)}, u32[]{:S(2)}, u32[]{:S(2)}) collective-permute-start(f16[3,3,2048]{2,1,0:T(4,128)(2,1)S(1)} %slice_select_fusion.1), channel_id=1, source_target_pairs={{0,1},{1,0},{2,3},{3,2},{4,5},{5,4},{6,7},{7,6},{8,9},{9,8},{10,11... | collective-permute-start | bytes 110600 | tf_op jit(solution)/shard_map/cond/branch_1_fun/ppermute | solution.py:45

commit v3 on v2

--- a/solution.py
+++ b/solution.py
@@ -225,7 +225,9 @@
     )
 
 
-def step_kernel(total_rows, where_ref, state_ref, depth_ref, wind_ref, out_ref, one, two, flux, done, sems):
+def step_kernel(
+    total_rows, where_ref, state_ref, depth_ref, wind_ref, out_ref, ends_ref, one, two, flux, done, sems
+):
     rows = state_ref.shape[1]
 
     def write(block):
@@ -236,6 +238,10 @@
         for part, value in enumerate(values):
             done[part, pl.ds(block * PAD, PAD), :] = value
         write(block).start()
+        for end, number in enumerate((0, rows // PAD - 1)):
+            if block == number:
+                for part, value in enumerate(values):
+                    ends_ref[end, part] = value
 
     first = where_ref[0] + PAD
     sections(
@@ -250,9 +256,12 @@
     vmem = pl.BlockSpec(memory_space=pltpu.VMEM)
     return pl.pallas_call(
         functools.partial(step_kernel, total_rows),
-        out_shape=jax.ShapeDtypeStruct((parts, rows, cols), jnp.float32),
+        out_shape=[
+            jax.ShapeDtypeStruct((parts, rows, cols), jnp.float32),
+            jax.ShapeDtypeStruct((2, parts, PAD, cols), jnp.float32),
+        ],
         in_specs=[pl.BlockSpec(memory_space=pltpu.SMEM), vmem, vmem, vmem],
-        out_specs=pl.BlockSpec(memory_space=pltpu.HBM),
+        out_specs=[pl.BlockSpec(memory_space=pltpu.HBM), vmem],
         scratch_shapes=[
             pltpu.VMEM((parts, rows, cols), jnp.float32),
             pltpu.VMEM((parts, rows, cols), jnp.float32),
@@ -270,25 +279,22 @@
 
 
 def edge_kernel(
-    total_rows, where_ref, above_ref, below_ref, depth_ref, wind_ref, old_ref, out_ref,
-    one, two, flux, done, kept, sems,
+    total_rows, where_ref, above_ref, below_ref, depth_ref, wind_ref, ends_ref, old_ref, out_ref,
+    one, two, flux, done, sem,
 ):
     rows = out_ref.shape[1]
     first = where_ref[0]
 
-    def edge(window, base, block, at, used):
+    def edge(window, base, block, end, at, used):
         here = pl.ds(at, PAD)
-        read = pltpu.make_async_copy(old_ref.at[:, here], kept, sems.at[0])
-        write = pltpu.make_async_copy(done, out_ref.at[:, here], sems.at[1])
-        read.start()
+        write = pltpu.make_async_copy(done, out_ref.at[:, here], sem)
 
         def store(number, values):
             if number != block:
                 return
-            read.wait()
             row = lax.broadcasted_iota(jnp.int32, (PAD, 1), 0)
             for part, value in enumerate(values):
-                done[part] = jnp.where(used(row), value, kept[part])
+                done[part] = jnp.where(used(row), value, ends_ref[end, part])
             write.start()
 
         sections(
@@ -298,14 +304,14 @@
 
     @pl.when(first + PAD > 0)
     def _():
-        edge(above_ref, 0, 1, 0, lambda row: row < EDGE)
+        edge(above_ref, 0, 1, 0, 0, lambda row: row < EDGE)
 
     @pl.when(first + PAD + rows < total_rows)
     def _():
-        edge(below_ref, rows, 0, rows - PAD, lambda row: row >= PAD - EDGE)
-
-
-def mend(result, above, below, depth, wind, first, total_rows):
+        edge(below_ref, rows, 0, 1, rows - PAD, lambda row: row >= PAD - EDGE)
+
+
+def mend(result, ends, above, below, depth, wind, first, total_rows):
     parts, rows, cols = result.shape
     vmem = pl.BlockSpec(memory_space=pltpu.VMEM)
     hbm = pl.BlockSpec(memory_space=pltpu.HBM)
@@ -313,24 +319,23 @@
     return pl.pallas_call(
         functools.partial(edge_kernel, total_rows),
         out_shape=jax.ShapeDtypeStruct((parts, rows, cols), jnp.float32),
-        in_specs=[pl.BlockSpec(memory_space=pltpu.SMEM), vmem, vmem, vmem, vmem, hbm],
+        in_specs=[pl.BlockSpec(memory_space=pltpu.SMEM), vmem, vmem, vmem, vmem, vmem, hbm],
         out_specs=hbm,
         scratch_shapes=[
             window,
             window,
             pltpu.VMEM((1, 2 * PAD, cols), jnp.float32),
             pltpu.VMEM((parts, PAD, cols), jnp.float32),
-            pltpu.VMEM((parts, PAD, cols), jnp.float32),
-            pltpu.SemaphoreType.DMA((2,)),
+            pltpu.SemaphoreType.DMA,
         ],
-        input_output_aliases={5: 0},
+        input_output_aliases={6: 0},
         compiler_params=pltpu.CompilerParams(vmem_limit_bytes=STEP_VMEM),
         cost_estimate=pl.CostEstimate(
             flops=200 * parts * PAD * cols,
             bytes_accessed=100 * parts * PAD * cols,
             transcendentals=0,
         ),
-    )(first[None].astype(jnp.int32), above, below, depth, wind, result)
+    )(first[None].astype(jnp.int32), above, below, depth, wind, ends, result)
 
 
 def exchange_all(cells, parents):
@@ -462,13 +467,13 @@
 
     def finish(parts, depth, stress):
         above, below = swap_edges(parts[0][:, :EDGE], parts[-1][:, -EDGE:])
-        result = step(
+        result, ends = step(
             jnp.concatenate([wide(part) for part in parts], axis=1), depth, stress, first, total_rows
         )
         above = [jnp.pad(wide(above), ((0, 0),) + fill[0]), wide(parts[0][:, :PAD])]
         below = [wide(parts[-1][:, -PAD:]), jnp.pad(wide(below), ((0, 0),) + fill[1])]
         above, below = [jnp.concatenate(window, axis=1) for window in (above, below)]
-        return mend(result, above, below, depth, stress, first, total_rows)
+        return mend(result, ends, above, below, depth, stress, first, total_rows)
 
     def far():
         around = surroundings(sea_depth, wind, start_hour)

time: 42.3 us -> 41.4 us (0.979)
  Pallas kernels: 7.5 us -> 6.68 us
    pallas_call x1, Pallas kernels: 2.06 us -> 1.23 us  [mend(): pl.pallas_call(functools.partial(edge_kernel, total_rows), out_shape=jax....]
where the time goes in v3:
time: 41.4 us; the launch traced here: 41.2 us
  starting transfers between devices  18 us (43%)
  other arithmetic  7.44 us (18%)
  Pallas kernels  6.68 us (16%)
  waiting for transfers between devices  5.27 us (13%)
  loops' own time  1.52 us (4%)
  local copies, waits for them, and re-layouts  1.4 us (3%)
  between operations  0.85 us (2%)
    ppermute x11, starting transfers between devices, move(): return lax.ppermute(array, 'dom', pairs) if pairs else array  14.4 us
    ppermute x11, waiting for transfers between devices, move(): return lax.ppermute(array, 'dom', pairs) if pairs else array  5.26 us
    pallas_call x1, Pallas kernels, step(): pl.pallas_call(functools.partial(step_kernel, total_rows), out_shape=[jax...  3.32 us
    pallas_call x1, Pallas kernels, fine_wind(): pl.pallas_call(wind_kernel, out_shape=jax.ShapeDtypeStruct((hours, parts,...  2.13 us
    ppermute x1, starting transfers between devices, surroundings(): sent.append(lax.ppermute(message, 'tile', pairs))  2.03 us
    ppermute x1, starting transfers between devices, swap_edges(): got = lax.ppermute(jnp.where(upper, tail, head), 'tile', pairs)  1.56 us
    another operation x1, loops' own time, body(): return lax.cond(close, near, far)[None]  1.52 us
    convert_element_type x1, other arithmetic, halves(): return (keep, send.astype(jnp.float16))  1.48 us
  transfers between devices with their start and end apart: 14, of which 4 were waited for; matrix products, arithmetic and copies ran while one was open for 13% of the time, Pallas kernels for 13%

profile of v3, /device:TPU:0, one launch (start us, length us, event | category | flops | bytes accessed | tf_op | source)
XLA Modules:
  0.0 41.2 jit_solution(16404864559304685973)
XLA Ops:
  0.0 0.8 %select_reduce_fusion.1 = s32[4]{0:T(128)S(1)} fusion(s32[16]{0:T(128)} %param.8, s32[4]{0:T(128)S(1)} %add_multiply_fusion), kind=kLoop, calls=%fused_computation.264 | loop fusion | flops 188 | bytes 96 | tf_op jit(solution)/shard_map/reduce_sum | solution.py:520
  0.8 0.6 %compare_reduce_fusion.3 = pred[]{:T(512)} fusion(s32[4]{0:T(128)S(1)} %select_reduce_fusion.1, s32[16]{0:T(128)S(1)} %iota.43), kind=kLoop, calls=%fused_computation.266 | loop fusion | flops 23 | bytes 33 | tf_op jit(solution)/shard_map/reduce_and | solution.py:521
  2.2 38.9 %conditional.1 = (f32[1,3,64,2048]{3,2,1,0:T(8,128)}) conditional(s32[]{:T(128)} %convert_element_type.232, (s32[]{:T(128)}, f32[1,3,64,2048]{3,2,1,0:T(8,128)}, s32[16]{0:T(128)}, s32[16]{0:T(128)S(1)}, s32[1]{0:T(128)}, /*index=5*/bf16[3,2,64,1024]{3,2,1,0:T(8,128)(2,1)}, f32[64,2048]{1,0:T(8,128)}) %tuple.16, (s32[]{:T(128)}, ...), branch_computations={%region_2.5_spmd, %region_5.10_spmd} | conditional | flops 120164016 | bytes 79011016 | solution.py:522
  2.2 1.5 %fusion.5 = (f16[3,32,2048]{2,1,0:T(8,128)(2,1)S(1)}, f32[3,32,2048]{2,1,0:T(8,128)S(1)}) fusion(f32[1,3,64,2048]{3,2,1,0:T(8,128)} %get-tuple-element.46, s32[]{:T(128)S(6)} %select_n.421, s32[]{:T(128)S(6)} %select_n.420), kind=kLoop, calls=%fused_computation.25 | loop fusion | flops 196608 | bytes 2752520 | tf_op jit(solution)/shard_map/cond/branch_1_fun/convert_element_type | solution.py:407
  3.7 0.5 %collective-permute-start = (f16[3,32,2048]{2,1,0:T(8,128)(2,1)S(1)}, f16[3,32,2048]{2,1,0:T(8,128)(2,1)S(1)}, u32[]{:S(2)}, u32[]{:S(2)}) collective-permute-start(f16[3,32,2048]{2,1,0:T(8,128)(2,1)S(1)} %get-tuple-element.48), channel_id=1, source_target_pairs={{0,2},{2,0},{4,6},{6,4},{8,10},{10,8},{12,14},{14,12},{16,18},{18,... | collective-permute-start | bytes 1179656 | tf_op jit(solution)/shard_map/cond/branch_1_fun/ppermute | solution.py:387
  5.9 0.7 %collective-permute-start.1 = (f16[2,3,16,2048]{3,2,1,0:T(8,128)(2,1)S(1)}, f16[2,3,16,2048]{3,2,1,0:T(8,128)(2,1)S(1)}, u32[]{:S(2)}, u32[]{:S(2)}) collective-permute-start(f16[2,3,16,2048]{3,2,1,0:T(8,128)(2,1)S(1)} %get-tuple-element.53), channel_id=1, source_target_pairs={{10,18},{14,22},{18,10},{22,14},{11,19},{15,23},{19,11},{23,15}} | collective-permute-start | bytes 1179656 | tf_op jit(solution)/shard_map/cond/branch_1_fun/ppermute | solution.py:387
  6.5 3.0 %collective-permute-start.2 = (f16[2,3,16,2048]{3,2,1,0:T(8,128)(2,1)S(1)}, f16[2,3,16,2048]{3,2,1,0:T(8,128)(2,1)S(1)}, u32[]{:S(2)}, u32[]{:S(2)}) collective-permute-start(f16[2,3,16,2048]{3,2,1,0:T(8,128)(2,1)S(1)} %get-tuple-element.53), channel_id=1, source_target_pairs={{0,4},{4,0},{8,12},{12,8},{16,20},{20,16},{24,28},{28,24},{2,10},{... | collective-permute-start | bytes 1179656 | tf_op jit(solution)/shard_map/cond/branch_1_fun/ppermute | solution.py:387
  9.5 0.7 %collective-permute-start.6 = (f16[2,3,16,2048]{3,2,1,0:T(8,128)(2,1)S(1)}, f16[2,3,16,2048]{3,2,1,0:T(8,128)(2,1)S(1)}, u32[]{:S(2)}, u32[]{:S(2)}) collective-permute-start(f16[2,3,16,2048]{3,2,1,0:T(8,128)(2,1)S(1)} %get-tuple-element.54), channel_id=1, source_target_pairs={{10,18},{14,22},{18,10},{22,14},{11,19},{15,23},{19,11},{23,15}} | collective-permute-start | bytes 1179656 | tf_op jit(solution)/shard_map/cond/branch_1_fun/ppermute | solution.py:387
  11.1 1.1 %constant_dynamic-slice_fusion = (bf16[1,2,40,1024]{3,2,1,0:T(8,128)(2,1)S(1)}, bf16[1,2,40,1024]{3,2,1,0:T(8,128)(2,1)S(1)}) fusion(bf16[3,2,64,1024]{3,2,1,0:T(8,128)(2,1)} %get-tuple-element.55, s32[]{:T(128)S(6)} %select_n.497, s32[]{:T(128)} %min.24, s32[]{:T(128)S(6)} %min.23), kind=kLoop, calls=%fused_computation.131 | loop fusion | bytes 655372 | tf_op jit(solution)/shard_map/cond/branch_1_fun/dynamic_slice | solution.py:79
  12.2 2.0 %collective-permute-start.10 = (bf16[92,1024]{1,0:T(8,128)(2,1)S(1)}, bf16[92,1024]{1,0:T(8,128)(2,1)S(1)}, u32[]{:S(2)}, u32[]{:S(2)}) collective-permute-start(bf16[92,1024]{1,0:T(8,128)(2,1)S(1)} %pad_maximum_fusion.1), channel_id=1, source_target_pairs={{0,1},{1,0},{2,3},{3,2},{4,5},{5,4},{6,7},{7,6},{8,9},{9,8},{10,11... | collective-permute-start | bytes 565256 | tf_op jit(solution)/shard_map/cond/branch_1_fun/ppermute | solution.py:91
  14.5 0.8 %collective-permute-done.2 = f16[2,3,16,2048]{3,2,1,0:T(8,128)(2,1)S(1)} collective-permute-done((f16[2,3,16,2048]{3,2,1,0:T(8,128)(2,1)S(1)}, f16[2,3,16,2048]{3,2,1,0:T(8,128)(2,1)S(1)}, u32[]{:S(2)}, u32[]{:S(2)}) %collective-permute-start.2) | collective-permute-done | bytes 393248 | tf_op jit(solution)/shard_map/cond/branch_1_fun/ppermute | solution.py:387
  15.3 0.5 %select_convert_fusion.5 = (f16[2,3,16,2048]{3,2,1,0:T(8,128)(2,1)S(1)}, f16[2,3,16,2048]{3,2,1,0:T(8,128)(2,1)S(1)}) fusion(f32[3,16,2048]{2,1,0:T(8,128)S(1)} %get-tuple-element.94, f32[3,16,2048]{2,1,0:T(8,128)S(1)} %get-tuple-element.93, f32[3,16,2048]{2,1,0:T(8,128)S(1)} %get-tuple-element.92, f32[3,16,2048]{2,1,0:T(8,128)S(1)} %get-tuple-element.91, ...), kind=kLoop, calls=%fused_computation.7 | loop fusion | flops 2359296 | bytes 3145748 | tf_op jit(solution)/shard_map/cond/branch_1_fun/convert_element_type | solution.py:505
  15.8 0.7 %collective-permute-start.3 = (f16[2,3,16,2048]{3,2,1,0:T(8,128)(2,1)S(1)}, f16[2,3,16,2048]{3,2,1,0:T(8,128)(2,1)S(1)}, u32[]{:S(2)}, u32[]{:S(2)}) collective-permute-start(f16[2,3,16,2048]{3,2,1,0:T(8,128)(2,1)S(1)} %get-tuple-element.69), channel_id=1, source_target_pairs={{8,16},{12,20},{16,8},{20,12},{9,17},{13,21},{17,9},{21,13}} | collective-permute-start | bytes 1179656 | tf_op jit(solution)/shard_map/cond/branch_1_fun/ppermute | solution.py:387
  16.5 4.9 %collective-permute-start.4 = (f16[2,3,16,2048]{3,2,1,0:T(8,128)(2,1)S(1)}, f16[2,3,16,2048]{3,2,1,0:T(8,128)(2,1)S(1)}, u32[]{:S(2)}, u32[]{:S(2)}) collective-permute-start(f16[2,3,16,2048]{3,2,1,0:T(8,128)(2,1)S(1)} %get-tuple-element.70), channel_id=1, source_target_pairs={{0,8},{4,12},{16,24},{20,28},{8,0},{12,4},{24,16},{28,20},{2,6},{6... | collective-permute-start | bytes 1179656 | tf_op jit(solution)/shard_map/cond/branch_1_fun/ppermute | solution.py:387
  21.7 0.6 %select_convert_fusion.1 = (f16[2,3,16,2048]{3,2,1,0:T(8,128)(2,1)S(1)}, f16[2,3,16,2048]{3,2,1,0:T(8,128)(2,1)S(1)}) fusion(f32[3,16,2048]{2,1,0:T(8,128)S(1)} %get-tuple-element.100, f32[3,16,2048]{2,1,0:T(8,128)S(1)} %get-tuple-element.99, f32[3,16,2048]{2,1,0:T(8,128)S(1)} %get-tuple-element.98, f32[3,16,2048]{2,1,0:T(8,128)S(1)} %get-tuple-element.97, ...), kind=kLoop, calls=%fused_computation.3 | loop fusion | flops 2752512 | bytes 3149844 | tf_op jit(solution)/shard_map/cond/branch_1_fun/convert_element_type | solution.py:505
  22.2 0.9 %collective-permute-start.9 = (f16[2,3,16,2048]{3,2,1,0:T(8,128)(2,1)S(1)}, f16[2,3,16,2048]{3,2,1,0:T(8,128)(2,1)S(1)}, u32[]{:S(2)}, u32[]{:S(2)}) collective-permute-start(f16[2,3,16,2048]{3,2,1,0:T(8,128)(2,1)S(1)} %get-tuple-element.67), channel_id=1, source_target_pairs={{8,16},{12,20},{16,8},{20,12},{9,17},{13,21},{17,9},{21,13}} | collective-permute-start | bytes 1179656 | tf_op jit(solution)/shard_map/cond/branch_1_fun/ppermute | solution.py:387
  23.3 2.8 %collective-permute-start.8 = (f16[2,3,16,2048]{3,2,1,0:T(8,128)(2,1)S(1)}, f16[2,3,16,2048]{3,2,1,0:T(8,128)(2,1)S(1)}, u32[]{:S(2)}, u32[]{:S(2)}) collective-permute-start(f16[2,3,16,2048]{3,2,1,0:T(8,128)(2,1)S(1)} %get-tuple-element.68), channel_id=1, source_target_pairs={{0,8},{4,12},{16,24},{20,28},{8,0},{12,4},{24,16},{28,20},{2,6},{6... | collective-permute-start | bytes 1179656 | tf_op jit(solution)/shard_map/cond/branch_1_fun/ppermute | solution.py:387
  26.3 2.1 %branch_1_fun.3.wind_ref = f32[2,2,80,2048]{3,2,1,0:T(8,128)S(1)} custom-call(s32[2]{0:T(128)S(1)} %pad_add_fusion.where_ref, bf16[160,1024]{1,0:T(8,128)(2,1)S(1)} %pad_maximum_fusion.coarse_ref), custom_call_target="tpu_custom_call" | custom-call | flops 52428800 | bytes 2621440 | tf_op jit(solution)/shard_map/cond/branch_1_fun/pallas_call | solution.py:148
  29.2 2.7 %collective-permute-done.8 = f16[2,3,16,2048]{3,2,1,0:T(8,128)(2,1)S(1)} collective-permute-done((f16[2,3,16,2048]{3,2,1,0:T(8,128)(2,1)S(1)}, f16[2,3,16,2048]{3,2,1,0:T(8,128)(2,1)S(1)}, u32[]{:S(2)}, u32[]{:S(2)}) %collective-permute-start.8) | collective-permute-done | bytes 393248 | tf_op jit(solution)/shard_map/cond/branch_1_fun/ppermute | solution.py:387
  32.0 0.5 %select_convert_fusion = f16[2,3,16,2048]{3,2,1,0:T(8,128)(2,1)S(1)} fusion(f32[3,16,2048]{2,1,0:T(8,128)S(1)} %get-tuple-element.88, f32[3,16,2048]{2,1,0:T(8,128)S(1)} %get-tuple-element.87, f32[3,16,2048]{2,1,0:T(8,128)S(1)} %get-tuple-element.86, f32[3,16,2048]{2,1,0:T(8,128)S(1)} %get-tuple-element.85, f32[3,16,2048]{2,1,0:T(8,128)S(1)} %get-tuple-element.100, ...), kind=kLoop, calls=%fused_computation.2 | loop fusion | flops 1966080 | bytes 4325394 | tf_op jit(solution)/shard_map/cond/branch_1_fun/convert_element_type | solution.py:448
  32.7 1.3 %collective-permute-done.12 = f16[3,16,2048]{2,1,0:T(8,128)(2,1)S(1)} collective-permute-done((f16[3,16,2048]{2,1,0:T(8,128)(2,1)S(1)}, f16[3,16,2048]{2,1,0:T(8,128)(2,1)S(1)}, u32[]{:S(2)}, u32[]{:S(2)}) %collective-permute-start.12) | collective-permute-done | bytes 196640 | tf_op jit(solution)/shard_map/cond/branch_1_fun/ppermute | solution.py:387
  34.2 1.6 %collective-permute-start.13 = (f16[3,3,2048]{2,1,0:T(4,128)(2,1)S(1)}, f16[3,3,2048]{2,1,0:T(4,128)(2,1)S(1)}, u32[]{:S(2)}, u32[]{:S(2)}) collective-permute-start(f16[3,3,2048]{2,1,0:T(4,128)(2,1)S(1)} %slice_select_fusion.1), channel_id=1, source_target_pairs={{0,1},{1,0},{2,3},{3,2},{4,5},{5,4},{6,7},{7,6},{8,9},{9,8},{10,11... | collective-permute-start | bytes 110600 | tf_op jit(solution)/shard_map/cond/branch_1_fun/ppermute | solution.py:45
  36.1 3.3 %branch_1_fun.4 = (f32[3,64,2048]{2,1,0:T(8,128)}, f32[2,3,8,2048]{3,2,1,0:T(8,128)S(1)}) custom-call(s32[1]{0:T(128)} %bitcast.27.where_ref, f32[3,64,2048]{2,1,0:T(8,128)S(1)} %maximum_convert_fusion.state_ref, f32[80,2048]{1,0:T(8,128)S(1)} %fusion.depth_ref, f32[2,2,80,2048]{3,2,1,0:T(8,128)S(1)} %branch_1_fun.3.wind_ref), custom_call_target="tpu_custom_call" | custom-call | flops 39321600 | bytes 6291456 | tf_op jit(solution)/shard_map/cond/branch_1_fun/pallas_call | solution.py:257
  39.6 1.2 %branch_1_fun.5 = f32[3,64,2048]{2,1,0:T(8,128)} custom-call(s32[1]{0:T(128)} %bitcast.27.where_ref, f32[3,16,2048]{2,1,0:T(8,128)S(1)} %fusion.11.above_ref, f32[3,16,2048]{2,1,0:T(8,128)S(1)} %fusion.9.below_ref, f32[80,2048]{1,0:T(8,128)S(1)} %fusion.depth_ref, f32[2,2,80,2048]{3,2,1,0:T(8,128)S(1)} %branch_1_fun.3.wind_ref, ...), custom_call_target="tpu_custom_call", output_to_operand_aliasing={{}: (6, {})} | custom-call | flops 9830400 | bytes 4915200 | tf_op jit(solution)/shard_map/cond/branch_1_fun/pallas_call | solution.py:319
  (73 shorter events, 4.0 us)
Async XLA Ops:
  3.7 1.9 %collective-permute-start = (f16[3,32,2048]{2,1,0:T(8,128)(2,1)S(1)}, f16[3,32,2048]{2,1,0:T(8,128)(2,1)S(1)}, u32[]{:S(2)}, u32[]{:S(2)}) collective-permute-start(f16[3,32,2048]{2,1,0:T(8,128)(2,1)S(1)} %get-tuple-element.48), channel_id=1, source_target_pairs={{0,2},{2,0},{4,6},{6,4},{8,10},{10,8},{12,14},{14,12},{16,18},{18,... | collective-permute-start | bytes 1179656 | tf_op jit(solution)/shard_map/cond/branch_1_fun/ppermute | solution.py:387
  5.1 5.2 %copy-start.3 = (s32[16]{0:T(128)S(1)}, s32[16]{0:T(128)}, u32[]{:S(2)}) copy-start(s32[16]{0:T(128)} %get-tuple-element.52) | copy-start | bytes 196 | tf_op jit(solution)/shard_map/cond
  5.6 5.4 %copy-start.1 = (f32[64,2048]{1,0:T(8,128)S(1)}, f32[64,2048]{1,0:T(8,128)}, u32[]{:S(2)}) copy-start(f32[64,2048]{1,0:T(8,128)} %get-tuple-element.57) | copy-start | bytes 1572868 | tf_op jit(solution)/shard_map/cond
  5.9 8.6 %collective-permute-start.1 = (f16[2,3,16,2048]{3,2,1,0:T(8,128)(2,1)S(1)}, f16[2,3,16,2048]{3,2,1,0:T(8,128)(2,1)S(1)}, u32[]{:S(2)}, u32[]{:S(2)}) collective-permute-start(f16[2,3,16,2048]{3,2,1,0:T(8,128)(2,1)S(1)} %get-tuple-element.53), channel_id=1, source_target_pairs={{10,18},{14,22},{18,10},{22,14},{11,19},{15,23},{19,11},{23,15}} | collective-permute-start | bytes 1179656 | tf_op jit(solution)/shard_map/cond/branch_1_fun/ppermute | solution.py:387
  6.5 8.7 %collective-permute-start.2 = (f16[2,3,16,2048]{3,2,1,0:T(8,128)(2,1)S(1)}, f16[2,3,16,2048]{3,2,1,0:T(8,128)(2,1)S(1)}, u32[]{:S(2)}, u32[]{:S(2)}) collective-permute-start(f16[2,3,16,2048]{3,2,1,0:T(8,128)(2,1)S(1)} %get-tuple-element.53), channel_id=1, source_target_pairs={{0,4},{4,0},{8,12},{12,8},{16,20},{20,16},{24,28},{28,24},{2,10},{... | collective-permute-start | bytes 1179656 | tf_op jit(solution)/shard_map/cond/branch_1_fun/ppermute | solution.py:387
  9.5 12.0 %collective-permute-start.6 = (f16[2,3,16,2048]{3,2,1,0:T(8,128)(2,1)S(1)}, f16[2,3,16,2048]{3,2,1,0:T(8,128)(2,1)S(1)}, u32[]{:S(2)}, u32[]{:S(2)}) collective-permute-start(f16[2,3,16,2048]{3,2,1,0:T(8,128)(2,1)S(1)} %get-tuple-element.54), channel_id=1, source_target_pairs={{10,18},{14,22},{18,10},{22,14},{11,19},{15,23},{19,11},{23,15}} | collective-permute-start | bytes 1179656 | tf_op jit(solution)/shard_map/cond/branch_1_fun/ppermute | solution.py:387
  10.2 11.4 %collective-permute-start.7 = (f16[2,3,16,2048]{3,2,1,0:T(8,128)(2,1)S(1)}, f16[2,3,16,2048]{3,2,1,0:T(8,128)(2,1)S(1)}, u32[]{:S(2)}, u32[]{:S(2)}) collective-permute-start(f16[2,3,16,2048]{3,2,1,0:T(8,128)(2,1)S(1)} %get-tuple-element.54), channel_id=1, source_target_pairs={{0,4},{4,0},{8,12},{12,8},{16,20},{20,16},{24,28},{28,24},{2,10},{... | collective-permute-start | bytes 1179656 | tf_op jit(solution)/shard_map/cond/branch_1_fun/ppermute | solution.py:387
  12.2 10.9 %collective-permute-start.10 = (bf16[92,1024]{1,0:T(8,128)(2,1)S(1)}, bf16[92,1024]{1,0:T(8,128)(2,1)S(1)}, u32[]{:S(2)}, u32[]{:S(2)}) collective-permute-start(bf16[92,1024]{1,0:T(8,128)(2,1)S(1)} %pad_maximum_fusion.1), channel_id=1, source_target_pairs={{0,1},{1,0},{2,3},{3,2},{4,5},{5,4},{6,7},{7,6},{8,9},{9,8},{10,11... | collective-permute-start | bytes 565256 | tf_op jit(solution)/shard_map/cond/branch_1_fun/ppermute | solution.py:91
  15.8 12.7 %collective-permute-start.3 = (f16[2,3,16,2048]{3,2,1,0:T(8,128)(2,1)S(1)}, f16[2,3,16,2048]{3,2,1,0:T(8,128)(2,1)S(1)}, u32[]{:S(2)}, u32[]{:S(2)}) collective-permute-start(f16[2,3,16,2048]{3,2,1,0:T(8,128)(2,1)S(1)} %get-tuple-element.69), channel_id=1, source_target_pairs={{8,16},{12,20},{16,8},{20,12},{9,17},{13,21},{17,9},{21,13}} | collective-permute-start | bytes 1179656 | tf_op jit(solution)/shard_map/cond/branch_1_fun/ppermute | solution.py:387
  16.5 12.1 %collective-permute-start.4 = (f16[2,3,16,2048]{3,2,1,0:T(8,128)(2,1)S(1)}, f16[2,3,16,2048]{3,2,1,0:T(8,128)(2,1)S(1)}, u32[]{:S(2)}, u32[]{:S(2)}) collective-permute-start(f16[2,3,16,2048]{3,2,1,0:T(8,128)(2,1)S(1)} %get-tuple-element.70), channel_id=1, source_target_pairs={{0,8},{4,12},{16,24},{20,28},{8,0},{12,4},{24,16},{28,20},{2,6},{6... | collective-permute-start | bytes 1179656 | tf_op jit(solution)/shard_map/cond/branch_1_fun/ppermute | solution.py:387
  22.2 9.7 %collective-permute-start.9 = (f16[2,3,16,2048]{3,2,1,0:T(8,128)(2,1)S(1)}, f16[2,3,16,2048]{3,2,1,0:T(8,128)(2,1)S(1)}, u32[]{:S(2)}, u32[]{:S(2)}) collective-permute-start(f16[2,3,16,2048]{3,2,1,0:T(8,128)(2,1)S(1)} %get-tuple-element.67), channel_id=1, source_target_pairs={{8,16},{12,20},{16,8},{20,12},{9,17},{13,21},{17,9},{21,13}} | collective-permute-start | bytes 1179656 | tf_op jit(solution)/shard_map/cond/branch_1_fun/ppermute | solution.py:387
  23.2 3.0 %collective-permute-start.11 = (bf16[80,1024]{1,0:T(8,128)(2,1)S(1)}, bf16[80,1024]{1,0:T(8,128)(2,1)S(1)}, u32[]{:S(2)}, u32[]{:S(2)}) collective-permute-start(bf16[80,1024]{1,0:T(8,128)(2,1)S(1)} %slice_select_fusion), channel_id=1, source_target_pairs={{0,2},{2,0},{4,6},{6,4},{8,10},{10,8},{12,14},{14,12},{16,18},{18,... | collective-permute-start | bytes 491528 | tf_op jit(solution)/shard_map/cond/branch_1_fun/ppermute | solution.py:116
  23.3 8.6 %collective-permute-start.8 = (f16[2,3,16,2048]{3,2,1,0:T(8,128)(2,1)S(1)}, f16[2,3,16,2048]{3,2,1,0:T(8,128)(2,1)S(1)}, u32[]{:S(2)}, u32[]{:S(2)}) collective-permute-start(f16[2,3,16,2048]{3,2,1,0:T(8,128)(2,1)S(1)} %get-tuple-element.68), channel_id=1, source_target_pairs={{0,8},{4,12},{16,24},{20,28},{8,0},{12,4},{24,16},{28,20},{2,6},{6... | collective-permute-start | bytes 1179656 | tf_op jit(solution)/shard_map/cond/branch_1_fun/ppermute | solution.py:387
  29.1 3.5 %collective-permute-start.5 = (f16[3,16,2048]{2,1,0:T(8,128)(2,1)S(1)}, f16[3,16,2048]{2,1,0:T(8,128)(2,1)S(1)}, u32[]{:S(2)}, u32[]{:S(2)}) collective-permute-start(f16[3,16,2048]{2,1,0:T(8,128)(2,1)S(1)} %slice_bitcast_fusion.7), channel_id=1, source_target_pairs={{0,2},{2,0},{4,6},{6,4},{8,10},{10,8},{12,14},{14,12},{16,18},{18,... | collective-permute-start | bytes 589832 | tf_op jit(solution)/shard_map/cond/branch_1_fun/ppermute | solution.py:387
  32.5 1.5 %collective-permute-start.12 = (f16[3,16,2048]{2,1,0:T(8,128)(2,1)S(1)}, f16[3,16,2048]{2,1,0:T(8,128)(2,1)S(1)}, u32[]{:S(2)}, u32[]{:S(2)}) collective-permute-start(f16[3,16,2048]{2,1,0:T(8,128)(2,1)S(1)} %slice_bitcast_fusion), channel_id=1, source_target_pairs={{0,2},{2,0},{4,6},{6,4},{8,10},{10,8},{12,14},{14,12},{16,18},{18,... | collective-permute-start | bytes 589832 | tf_op jit(solution)/shard_map/cond/branch_1_fun/ppermute | solution.py:387
  34.2 5.2 %collective-permute-start.13 = (f16[3,3,2048]{2,1,0:T(4,128)(2,1)S(1)}, f16[3,3,2048]{2,1,0:T(4,128)(2,1)S(1)}, u32[]{:S(2)}, u32[]{:S(2)}) collective-permute-start(f16[3,3,2048]{2,1,0:T(4,128)(2,1)S(1)} %slice_select_fusion.1), channel_id=1, source_target_pairs={{0,1},{1,0},{2,3},{3,2},{4,5},{5,4},{6,7},{7,6},{8,9},{9,8},{10,11... | collective-permute-start | bytes 110600 | tf_op jit(solution)/shard_map/cond/branch_1_fun/ppermute | solution.py:45
